TPU v7x, 32 devices: a whole 2x2x4 slice. The times are simulated.
32 devices in a mesh: space: 8 (over z, x), sample: 4 (over y, core).
Axes of the slice: x: 2, y: 2, z: 4, core: 2. Of those that a mesh axis runs over, the one named last changes fastest.
Arguments:
- crops: bfloat16 [32, 16, 16, 1024], P('sample', None, 'space'), may hold values from -6 to 6
- first_kernel: bfloat16 [32, 16, 3, 3, 3], replicated, may hold values from -0.3125 to 0.3125
- second_kernel: bfloat16 [64, 32, 3, 3, 3], replicated, may hold values from -0.21875 to 0.21875
- out_grad: bfloat16 [32, 64, 4, 64], P(('sample', 'space')), may hold values from -0.15625 to 0.15625
Outputs:
- features_out: bfloat16 [32, 64, 4, 64], P(('sample', 'space'))
- first_grad: float32 [32, 16, 3, 3, 3], replicated
- second_grad: float32 [64, 32, 3, 3, 3], replicated
All inputs are finite; a program needn't handle non-finite values.
Results may differ from a plain program's by a relative error of at most 0.012.
Values may be sent and summed in bfloat16 or wider, within the bound.
No kernel may reach another device: no remote copies, remote signals or barrier semaphores. Data moves between devices by JAX's collectives and lax.ppermute only.
A program may use at most 128 MiB of HBM per device.

v0:
```python
import functools
import math

import jax
import jax.numpy as jnp
from jax import lax
from jax.experimental import pallas as pl
from jax.experimental.pallas import tpu as pltpu
from jax.sharding import PartitionSpec as P

HEIGHT = 8
WIDTH = 128
LANES = 128
VMEM_BYTES = 16 * 1024 * 1024
TERM_ROWS = 576


def iota(shape, dim):
    return lax.broadcasted_iota(jnp.int32, shape, dim)


def dot(left, right, dims=((1,), (0,))):
    return lax.dot_general(left, right, (dims, ((), ())), preferred_element_type=jnp.float32)


def ones_where(mask):
    return jnp.where(mask, 1.0, 0.0).astype(jnp.bfloat16)


def band_of_second(k2_ref, k2t_ref):
    channels_mid, channels_out = k2_ref.shape[3:]
    empty = jnp.zeros((channels_mid, channels_out), jnp.bfloat16)
    for ad in range(3):
        for aw in range(3):
            tap = [k2_ref[ad, ah, aw] for ah in range(3)]
            band = ((tap[1], empty), (tap[2], tap[0]), (empty, tap[1]), (empty, tap[2]))
            start = (ad * 3 + aw) * 2 * channels_out
            for hh in range(4):
                k2t_ref[hh * channels_mid:(hh + 1) * channels_mid, start:start + 2 * channels_out] = (
                    jnp.concatenate(band[hh], axis=1))


def upsampling(ad, aw, beyond=0):
    row, col = iota((128, 512), 0), iota((128, 512), 1)
    target = ((row >> 5) << 7) + ((row & 31) << 1) + (64 * (ad - 1) + aw - 1 + 128 * beyond)
    keep = col == target
    if aw == 0:
        keep = keep & ((row & 31) > 0)
    return ones_where(keep)


def prepare_kernel(k1_ref, k2_ref, og_ref, pick_ref, k1t_ref, ogt_ref, ag_ref, k2t_ref, ogu_ref):
    channels_in, channels_mid = k1_ref.shape[3:]
    row, col = iota((3 * WIDTH, 2 * 64), 0), iota((3 * WIDTH, 2 * 64), 1)
    for aw in range(3):
        same = ((row >> 7) & 1) == (col >> 6)
        tap = (row & 127) == 2 * (col & 63) + aw - 1
        pick_ref[:, aw * 128:(aw + 1) * 128] = ones_where(same & tap)
    shape = (9 * channels_in, channels_in * 2 * HEIGHT)
    row, col = iota(shape, 0), iota(shape, 1)
    tap = row >> 4
    ad = jnp.where(tap >= 6, 2, jnp.where(tap >= 3, 1, 0))
    ah, i = tap - 3 * ad, row & 15
    same = i == col >> 4
    h, d = (col >> 1) & 7, col & 1
    taps = []
    for aw in range(3):
        parts = [k1_ref[a, b, aw] for a in range(3) for b in range(3)]
        taps.append(jnp.concatenate(parts, axis=0).astype(jnp.float32).T.astype(jnp.bfloat16))
    for following in range(2):
        plane = (ad == 0) & (d == 1) if following else (ad == d + 1)
        for hh in range(4):
            place = ones_where(same & plane & (h == 2 * hh + ah - 1))
            start = (following * 4 + hh) * channels_mid
            for aw in range(3):
                block = dot(taps[aw], place).astype(jnp.bfloat16)
                k1t_ref[start:start + channels_mid, aw * shape[1]:(aw + 1) * shape[1]] = block
    band_of_second(k2_ref, k2t_ref)
    groups = og_ref.shape[1] // 128
    for ad in range(3):
        for aw in range(3):
            t = ad * 3 + aw
            up = upsampling(ad, aw)
            for g in range(groups):
                value = dot(og_ref[:, g * 128:(g + 1) * 128], up)
                if ad == 0 and g + 1 < groups:
                    value = value + dot(og_ref[:, (g + 1) * 128:(g + 2) * 128], upsampling(ad, aw, 4))
                ogu_ref[t * 128:(t + 1) * 128, g * 512:(g + 1) * 512] = value.astype(jnp.bfloat16)
                ogt_ref[g * 512:(g + 1) * 512, t * 128:(t + 1) * 128] = value.T.astype(jnp.bfloat16)
    for g in range(groups):
        lanes = slice(g * 512, (g + 1) * 512)
        ag_ref[:, lanes] = dot(k2t_ref[...], ogu_ref[:, lanes]).astype(jnp.bfloat16)


def taps_of_pair(first_ref, second_ref, pick_ref):
    parity = lax.axis_index("space") & 1
    pick = pick_ref[pl.ds(pl.multiple_of(parity * WIDTH, WIDTH), 2 * WIDTH), :]
    pair = jnp.concatenate([first_ref[...], second_ref[...]], axis=1)
    return dot(pair, pick).astype(jnp.bfloat16)


def taps_kernel(pairs, given, *refs):
    pick_ref, out_ref = refs[-2:]
    for place, m in enumerate(pairs):
        y = taps_of_pair(refs[given.index(2 * m)], refs[given.index(2 * m + 1)], pick_ref)
        for aw in range(3):
            out_ref[aw * 256:(aw + 1) * 256, place * 128:(place + 1) * 128] = y[:, aw * 128:(aw + 1) * 128]


def layer_kernel(pairs, y_ref, first_ref, second_ref, pick_ref, k1t_ref, ogt_ref, ag_ref, act_ref, terms_ref, y_scr, pg_scr):
    cells = ag_ref.shape[1]
    rows = 256
    here = lax.axis_index("space") >> 1
    for place, m in enumerate(pairs):
        lanes = pl.ds(pl.multiple_of(lax.bitwise_xor(here, jnp.int32(m)) * 128, 128), 128)
        if place + 1 < len(pairs):
            y_scr[:, lanes] = y_ref[:, place * 128:(place + 1) * 128]
            continue
        y = taps_of_pair(first_ref, second_ref, pick_ref)
        for aw in range(3):
            y_scr[aw * rows:(aw + 1) * rows, lanes] = y[:, aw * 128:(aw + 1) * 128]
    both = dot(k1t_ref[...], y_scr[...])
    lane = iota((128, cells), 1)
    from_last = jnp.where(lane < 64, 0.0, pltpu.roll(both[128:], 64, 1))
    pre = both[:128] + from_last
    sigma = jax.nn.sigmoid(pre)
    act = (pre * sigma).astype(jnp.bfloat16)
    act_ref[...] = act
    slope = sigma * (1.0 + pre * (1.0 - sigma))
    grad = (ag_ref[...].astype(jnp.float32) * slope).astype(jnp.bfloat16)
    pg_scr[:128, :] = grad
    to_last = pltpu.roll(grad.astype(jnp.float32), cells - 64, 1)
    pg_scr[128:, :] = jnp.where(lane < cells - 64, to_last, 0.0).astype(jnp.bfloat16)

    second = dot(act, ogt_ref[...])
    lane = iota((32, 128), 1)
    held = None
    for t in range(9):
        tile = second[:, t * 128:(t + 1) * 128]
        turned = pltpu.roll(tile, 64, 1)
        mixed = jnp.where(lane < 64, tile[0:32] + turned[64:96], turned[32:64] + tile[96:128])
        terms_ref[t * 32:(t + 1) * 32, :] = mixed.astype(jnp.bfloat16)
        if t % 2 == 0:
            held = jnp.where(lane < 64, turned[32:64], 0.0)
        else:
            held = jnp.where(lane < 64, held, tile[32:64])
        if t % 2 == 1:
            start = 288 + (t // 2) * 32
            terms_ref[start:start + 32, :] = held.astype(jnp.bfloat16)
    terms_ref[416:432, :] = jnp.where(lane[:16] < 64, held[:16], pltpu.roll(held[16:], 64, 1)).astype(jnp.bfloat16)

    first = dot(y_scr[...], pg_scr[...], ((1,), (1,))).astype(jnp.bfloat16)
    shape = (rows, 256)
    h, hh = (iota(shape, 0) >> 1) & 7, (iota(shape, 1) >> 5) & 3
    even, odd = ones_where((h >> 1) == hh), ones_where(((h & 1) == 1) & ((h + 1) >> 1 == hh))
    rank, index = iota((64, rows), 0), iota((64, rows), 1)
    same = ((rank & 15) == index >> 4) & (((rank >> 4) & 1) == (index & 1))
    later_taps = ones_where(same & ((rank >> 5) == ((index >> 1) & 1)))
    first_tap = ones_where(same[:32] & (((index[:32] >> 1) & 1) == 1))
    lane = iota((16, 128), 1)
    for aw in range(3):
        tile = first[aw * rows:(aw + 1) * rows]
        total = jnp.concatenate([dot(first_tap, tile * odd), dot(later_taps, tile * even)], axis=0)
        start = 432 + aw * 48
        for ad in range(3):
            side = slice(128, 256) if ad == 0 else slice(0, 128)
            d = 0 if ad == 1 else 1
            packed = None
            for ah in range(3):
                part = total[ah * 32 + d * 16:ah * 32 + d * 16 + 16, side]
                part = part + pltpu.roll(part, 64, 1)
                part = part + pltpu.roll(part, 32, 1)
                packed = part if packed is None else jnp.where(lane >= ah * 32, part, packed)
            terms_ref[start + ad * 16:start + (ad + 1) * 16, :] = packed.astype(jnp.bfloat16)
    rest = terms_ref.shape[0] - TERM_ROWS
    if rest > 0:
        terms_ref[TERM_ROWS:, :] = jnp.zeros((rest, 128), jnp.bfloat16)


def features_kernel(act_ref, k2_ref, out_ref, k2t_ref):
    band_of_second(k2_ref, k2t_ref)
    groups = out_ref.shape[1] // 128
    for g in range(groups):
        total = jnp.zeros((128, 128), jnp.float32)
        for t in range(9):
            taken = dot(act_ref[:, g * 512:(g + 1) * 512], upsampling(t // 3, t % 3), ((1,), (1,)))
            if t < 3 and g > 0:
                last = act_ref[:, (g - 1) * 512:g * 512]
                taken = taken + dot(last, upsampling(0, t, 4), ((1,), (1,)))
            band = k2t_ref[:, t * 128:(t + 1) * 128]
            total = total + dot(band, taken.astype(jnp.bfloat16), ((0,), (0,)))
        out_ref[:, g * 128:(g + 1) * 128] = total.astype(jnp.bfloat16)


def add_kernel(rows, mine_ref, out_ref):
    count = mine_ref.shape[0]
    unit = rows * 16 // math.gcd(rows, 16)
    total = mine_ref[0:unit, :].astype(jnp.float32)
    for start in range(unit, count, unit):
        total = total + mine_ref[start:start + unit, :].astype(jnp.float32)
    if unit % (2 * rows) == 0 and (unit // 2) % 8 == 0:
        total = total[:unit // 2] + total[unit // 2:]
    parts = [total[start:start + rows] for start in range(0, total.shape[0], rows)]
    total = functools.reduce(jnp.add, parts)
    spread = jnp.concatenate([total] * (unit // rows), axis=0).astype(jnp.bfloat16)
    for start in range(0, count, unit):
        out_ref[start:start + unit, :] = spread


def unpack_kernel(whole_ref, first_ref, second_ref, first_scr, second_scr, sems):
    copies = []
    for ad in range(3):
        for aw in range(3):
            t = ad * 3 + aw
            pair = whole_ref[t * 32:(t + 1) * 32, :].astype(jnp.float32)
            second_scr[ad, 1, aw] = pair[:, :64]
            second_scr[ad, 2, aw] = pair[:, 64:]
            if t == 8:
                lone = whole_ref[416:432, :].astype(jnp.float32)
                second_scr[ad, 0, aw] = jnp.concatenate([lone[:, :64], lone[:, 64:]], axis=0)
            else:
                start = 288 + (t // 2) * 32
                lone = whole_ref[start:start + 32, :].astype(jnp.float32)
                second_scr[ad, 0, aw] = lone[:, :64] if t % 2 == 0 else lone[:, 64:]
        copies.append(pltpu.make_async_copy(second_scr.at[ad], second_ref.at[ad], sems.at[0, ad]))
        copies[-1].start()
    for ad in range(3):
        for aw in range(3):
            start = 432 + aw * 48 + ad * 16
            tile = whole_ref[start:start + 16, :].astype(jnp.float32)
            for ah in range(3):
                first_scr[ad, ah, aw] = tile[:, ah * 32:(ah + 1) * 32]
        copies.append(pltpu.make_async_copy(first_scr.at[ad], first_ref.at[ad], sems.at[1, ad]))
        copies[-1].start()
    for copy in copies:
        copy.wait()


def call(kernel, outs, args, scratch=(), flops=0):
    whole = pl.BlockSpec(memory_space=pltpu.VMEM)
    scalar = pl.BlockSpec(memory_space=pltpu.SMEM)
    size = sum(a.size * a.dtype.itemsize for a in list(args) + list(outs))
    return pl.pallas_call(
        kernel,
        out_shape=tuple(outs),
        in_specs=[scalar if a.dtype == jnp.int32 else whole for a in args],
        out_specs=(whole,) * len(outs),
        scratch_shapes=list(scratch),
        compiler_params=pltpu.CompilerParams(vmem_limit_bytes=VMEM_BYTES),
        cost_estimate=pl.CostEstimate(flops=flops, bytes_accessed=size, transcendentals=0),
    )(*args)


def array(shape, dtype=jnp.bfloat16):
    return jax.ShapeDtypeStruct(shape, dtype)


def by_tap(kernel):
    return jnp.transpose(kernel, (2, 3, 4, 1, 0))


def prepare(k1, k2, out_grad):
    c0, c1 = k1.shape[3:]
    c2 = k2.shape[4]
    planes = out_grad.shape[2]
    cells = planes * 2 * 64
    og = out_grad.reshape(c2, planes, 2, 32).transpose(2, 0, 1, 3).reshape(2 * c2, planes * 32)
    outs = [
        array((384, 384)),
        array((2 * 4 * c1, 3 * c0 * 16)),
        array((cells, 9 * 2 * c2)),
        array((4 * c1, cells)),
    ]
    scratch = [pltpu.VMEM((4 * c1, 9 * 2 * c2), jnp.bfloat16), pltpu.VMEM((9 * 2 * c2, cells), jnp.bfloat16)]
    return call(prepare_kernel, outs, (k1, k2, og), scratch, flops=2 * 128 * 1152 * cells * 2)


def body(crops, first_kernel, second_kernel, out_grad):
    axes = ("space", "sample")
    devices = lax.axis_size(axes)
    channels_out, planes = out_grad.shape[1:3]
    space = lax.axis_size("space")
    assert space & (space - 1) == 0
    position = lax.axis_index("space").astype(jnp.int32)
    across = list(range(space - 1, space // 2 - 1, -1))
    order = across[:1] + [1] + across[1:] + list(range(4, space // 2)) + [2, 3]
    early, late = order[:space // 2], order[space // 2:]
    last = 1
    pairs = [m for m in range(space // 2) if m != last] + [last]
    k1, k2 = by_tap(first_kernel), by_tap(second_kernel)
    x = {}
    cut = [lax.dynamic_index_in_dim(crops, position ^ step, 0, keepdims=False) for step in early]
    rest, cut = lax.optimization_barrier((crops, cut))
    for step in [0] + late[::-1] + early:
        if step in early:
            block = cut[early.index(step)]
        else:
            block = lax.dynamic_index_in_dim(rest, position ^ step, 0, keepdims=False)
        if step > 0:
            block = lax.ppermute(block, "space", [(source, source ^ step) for source in range(space)])
        channels_in, two, flat_cells = block.shape
        block = block.reshape(channels_in, two, HEIGHT, WIDTH).transpose(0, 2, 1, 3)
        x[step] = block.reshape(channels_in * two * HEIGHT, WIDTH)
    pick, k1t, ogt, act_grad = prepare(k1, k2, out_grad)
    cells = act_grad.shape[1]
    given = early + [step for step in x if step not in early and step // 2 != last]
    (y,) = call(
        functools.partial(taps_kernel, pairs[:-1], given),
        [array((768, cells - 128))],
        [x[step] for step in given] + [pick],
        flops=2 * 256 * 384 * cells,
    )
    rows = -(-TERM_ROWS // (devices * 2)) * 2
    act, terms = call(
        functools.partial(layer_kernel, pairs),
        [array((128, cells)), array((devices * rows, LANES))],
        (y, x[2 * last], x[2 * last + 1], pick, k1t, ogt, act_grad),
        scratch=[pltpu.VMEM((768, cells), jnp.bfloat16), pltpu.VMEM((256, cells), jnp.bfloat16)],
        flops=2 * 128 * 4096 * cells,
    )
    blocks = terms.reshape(devices, rows // 2, 2, LANES)
    mine = lax.all_to_all(blocks, axes, split_axis=0, concat_axis=0, tiled=True)
    (features,) = call(
        features_kernel,
        [array((2 * channels_out, planes * 32))],
        (act, k2),
        scratch=[pltpu.VMEM((128, 1152), jnp.bfloat16)],
        flops=2 * 128 * 1152 * cells,
    )
    features = features.reshape(2, channels_out, planes, 32).transpose(1, 2, 0, 3).reshape(out_grad.shape)
    add = functools.partial(add_kernel, rows)
    (spread,) = call(add, [array(terms.shape)], (mine.reshape(terms.shape),))
    spread = spread.reshape(blocks.shape)
    whole = lax.all_to_all(spread, axes, split_axis=0, concat_axis=0, tiled=True)
    shapes = [(3, 3, 3) + kernel.shape[1::-1] for kernel in (first_kernel, second_kernel)]
    first, second = pl.pallas_call(
        unpack_kernel,
        out_shape=[array(shape, jnp.float32) for shape in shapes],
        in_specs=[pl.BlockSpec(memory_space=pltpu.VMEM)],
        out_specs=[pl.BlockSpec(memory_space=pl.ANY)] * 2,
        scratch_shapes=[pltpu.VMEM(shape, jnp.float32) for shape in shapes] + [pltpu.SemaphoreType.DMA((2, 3))],
        compiler_params=pltpu.CompilerParams(vmem_limit_bytes=VMEM_BYTES),
    )(whole.reshape(terms.shape))
    return (features, jnp.transpose(first, (4, 3, 0, 1, 2)), jnp.transpose(second, (4, 3, 0, 1, 2)))


def solution(mesh):
    placed = (P("sample", None, "space", None), P(), P(), P(("sample", "space"), None, None, None))
    return jax.shard_map(
        body,
        mesh=mesh,
        in_specs=placed,
        out_specs=(P(("sample", "space"), None, None, None), P(), P()),
        check_vma=False,
    )
```

profile of v0, /device:TPU:0, one launch (start us, length us, event | category | flops | bytes accessed | tf_op | source)
XLA Modules:
  0.0 48.0 jit_solution(7653394797463005550)
XLA Ops:
  0.7 1.2 %dynamic-slice_bitcast_fusion.3 = (bf16[16,2,1024]{2,1,0:T(2,128)(2,1)S(1)}, bf16[16,2,1024]{2,1,0:T(2,128)(2,1)S(1)}, bf16[16,2,1024]{2,1,0:T(2,128)(2,1)S(1)}, bf16[16,2,1024]{2,1,0:T(2,128)(2,1)S(1)}) fusion(bf16[8,16,2,1024]{3,2,1,0:T(2,128)(2,1)} %param.4, s32[]{:T(128)S(6)} %select_n.28, s32[]{:T(128)S(6)} %select_n.27, s32[]{:T(128)S(6)} %select_n.26, ...), kind=kLoop, calls=%fused_computation.3 | loop fusion | bytes 524304 | tf_op jit(solution)/shard_map/jit(dynamic_index_in_dim)/squeeze | solution.py:292
  1.9 6.0 %collective-permute-start = (bf16[16,2,1024]{2,1,0:T(2,128)(2,1)S(1)}, bf16[16,2,1024]{2,1,0:T(2,128)(2,1)S(1)}, u32[]{:S(2)}, u32[]{:S(2)}) collective-permute-start(bf16[16,2,1024]{2,1,0:T(2,128)(2,1)S(1)} %get-tuple-element.16), channel_id=1, source_target_pairs={{0,28},{4,24},{8,20},{12,16},{16,12},{20,8},{24,4},{28,0},{1,29},{... | collective-permute-start | bytes 196616 | tf_op jit(solution)/shard_map/ppermute | solution.py:300
  7.9 0.5 %collective-permute-start.1 = (bf16[16,2,1024]{2,1,0:T(2,128)(2,1)S(1)}, bf16[16,2,1024]{2,1,0:T(2,128)(2,1)S(1)}, u32[]{:S(2)}, u32[]{:S(2)}) collective-permute-start(bf16[16,2,1024]{2,1,0:T(2,128)(2,1)S(1)} %get-tuple-element.17), channel_id=1, source_target_pairs={{0,4},{4,0},{8,12},{12,8},{16,20},{20,16},{24,28},{28,24},{1,5},{5... | collective-permute-start | bytes 196616 | tf_op jit(solution)/shard_map/ppermute | solution.py:300
  8.6 1.8 %collective-permute-start.3 = (bf16[16,2,1024]{2,1,0:T(2,128)(2,1)S(1)}, bf16[16,2,1024]{2,1,0:T(2,128)(2,1)S(1)}, u32[]{:S(2)}, u32[]{:S(2)}) collective-permute-start(bf16[16,2,1024]{2,1,0:T(2,128)(2,1)S(1)} %get-tuple-element.19), channel_id=1, source_target_pairs={{0,20},{4,16},{8,28},{12,24},{16,4},{20,0},{24,12},{28,8},{1,21},{... | collective-permute-start | bytes 196616 | tf_op jit(solution)/shard_map/ppermute | solution.py:300
  10.4 1.1 %dynamic-slice_bitcast_fusion = (bf16[16,2,1024]{2,1,0:T(2,128)(2,1)S(1)}, bf16[16,2,1024]{2,1,0:T(2,128)(2,1)S(1)}, bf16[16,2,1024]{2,1,0:T(2,128)(2,1)S(1)}, bf16[1,16,2,1024]{3,2,1,0:T(2,128)(2,1)S(1)}) fusion(bf16[8,16,2,1024]{3,2,1,0:T(2,128)(2,1)} %param.4, s32[]{:T(128)S(6)} %select_n.32, s32[]{:T(128)S(6)} %select_n.31, s32[]{:T(128)S(6)} %select_n.30, ...), kind=kLoop, calls=%fused_computation | loop fusion | bytes 524304 | tf_op jit(solution)/shard_map/jit(dynamic_index_in_dim)/squeeze | solution.py:298
  11.5 2.2 %collective-permute-start.4 = (bf16[16,2,1024]{2,1,0:T(2,128)(2,1)S(1)}, bf16[16,2,1024]{2,1,0:T(2,128)(2,1)S(1)}, u32[]{:S(2)}, u32[]{:S(2)}) collective-permute-start(bf16[16,2,1024]{2,1,0:T(2,128)(2,1)S(1)} %get-tuple-element.34), channel_id=1, source_target_pairs={{0,16},{4,20},{8,24},{12,28},{16,0},{20,4},{24,8},{28,12},{1,17},{... | collective-permute-start | bytes 196616 | tf_op jit(solution)/shard_map/ppermute | solution.py:300
  13.7 1.3 %collective-permute-start.6 = (bf16[16,2,1024]{2,1,0:T(2,128)(2,1)S(1)}, bf16[16,2,1024]{2,1,0:T(2,128)(2,1)S(1)}, u32[]{:S(2)}, u32[]{:S(2)}) collective-permute-start(bf16[16,2,1024]{2,1,0:T(2,128)(2,1)S(1)} %get-tuple-element.32), channel_id=1, source_target_pairs={{0,12},{4,8},{8,4},{12,0},{16,28},{20,24},{24,20},{28,16},{1,13},{... | collective-permute-start | bytes 196616 | tf_op jit(solution)/shard_map/ppermute | solution.py:300
  15.0 0.6 %collective-permute-start.5 = (bf16[16,2,1024]{2,1,0:T(2,128)(2,1)S(1)}, bf16[16,2,1024]{2,1,0:T(2,128)(2,1)S(1)}, u32[]{:S(2)}, u32[]{:S(2)}) collective-permute-start(bf16[16,2,1024]{2,1,0:T(2,128)(2,1)S(1)} %get-tuple-element.33), channel_id=1, source_target_pairs={{0,8},{4,12},{8,0},{12,4},{16,24},{20,28},{24,16},{28,20},{1,9},{5... | collective-permute-start | bytes 196616 | tf_op jit(solution)/shard_map/ppermute | solution.py:300
  15.9 0.1 copy.11.og_ref
  16.0 1.3 %shard_map.67 = (bf16[384,384]{1,0:T(8,128)(2,1)S(1)}, bf16[256,768]{1,0:T(8,128)(2,1)S(1)}, bf16[512,1152]{1,0:T(8,128)(2,1)S(1)}, bf16[128,512]{1,0:T(8,128)(2,1)S(1)}) custom-call(bf16[3,3,3,16,32]{4,3,2,1,0:T(8,128)(2,1)S(1)} %bitcast.84, bf16[3,3,3,32,64]{4,3,2,1,0:T(8,128)(2,1)S(1)} %bitcast.82, bf16[128,128]{1,0:T(8,128)(2,1)S(1)} %copy.11.og_ref), custom_call_target="tpu_custom_call" | custom-call | flops 301989888 | bytes 2169856 | tf_op jit(solution)/shard_map/pallas_call | solution.py:243
  17.3 0.9 %collective-permute-done.3 = bf16[16,2,1024]{2,1,0:T(2,128)(2,1)S(1)} collective-permute-done((bf16[16,2,1024]{2,1,0:T(2,128)(2,1)S(1)}, bf16[16,2,1024]{2,1,0:T(2,128)(2,1)S(1)}, u32[]{:S(2)}, u32[]{:S(2)}) %collective-permute-start.3) | collective-permute-done | bytes 65568 | tf_op jit(solution)/shard_map/ppermute | solution.py:300
  18.2 0.4 collective-permute-done.4
  18.6 0.4 shard_map.68.y_ref
  19.0 1.1 %collective-permute-done.6 = bf16[16,2,1024]{2,1,0:T(2,128)(2,1)S(1)} collective-permute-done((bf16[16,2,1024]{2,1,0:T(2,128)(2,1)S(1)}, bf16[16,2,1024]{2,1,0:T(2,128)(2,1)S(1)}, u32[]{:S(2)}, u32[]{:S(2)}) %collective-permute-start.6) | collective-permute-done | bytes 65568 | tf_op jit(solution)/shard_map/ppermute | solution.py:300
  20.1 0.1 collective-permute-done.5
  20.2 1.7 %shard_map.69 = (bf16[128,512]{1,0:T(8,128)(2,1)S(1)}, bf16[576,128]{1,0:T(8,128)(2,1)S(1)}) custom-call(bf16[768,384]{1,0:T(8,128)(2,1)S(1)} %shard_map.68.y_ref, bf16[256,128]{1,0:T(8,128)(2,1)S(1)} %bitcast.81, bf16[256,128]{1,0:T(8,128)(2,1)S(1)} %bitcast.79, bf16[384,384]{1,0:T(8,128)(2,1)S(1)} %get-tuple-element.21.refs_6_.pick_ref, ...), custom_call_target="tpu_custom_call" | custom-call | flops 536870912 | bytes 2998272 | tf_op jit(solution)/shard_map/pallas_call | solution.py:243
  21.9 13.4 %all_to_all.10 = bf16[32,9,2,128]{3,2,1,0:T(2,128)(2,1)S(1)} all-to-all(bf16[32,9,2,128]{3,2,1,0:T(2,128)(2,1)S(1)} %bitcast.74), channel_id=1, replica_groups=mesh['space'=8,'sample'=4] {'space','sample'}, dimensions={0} | all-to-all | bytes 294912 | tf_op jit(solution)/shard_map/all_to_all | solution.py:322
  35.3 0.7 %shard_map.71 = bf16[576,128]{1,0:T(8,128)(2,1)} custom-call(bf16[576,128]{1,0:T(8,128)(2,1)S(1)} %bitcast.72), custom_call_target="tpu_custom_call" | custom-call | bytes 294912 | tf_op jit(solution)/shard_map/pallas_call | solution.py:243
  36.0 2.6 %all-to-all-start.1 = ((bf16[32,9,2,128]{3,2,1,0:T(2,128)(2,1)}), bf16[32,9,2,128]{3,2,1,0:T(2,128)(2,1)S(1)}, u32[]{:S(2)}, u32[]{:S(2)}) async-start(bf16[32,9,2,128]{3,2,1,0:T(2,128)(2,1)} %bitcast.39), calls=%async_computation.1 | async-start | bytes 294912 | tf_op jit(solution)/shard_map/all_to_all | solution.py:334
  38.6 1.0 %shard_map.70 = bf16[128,128]{1,0:T(8,128)(2,1)S(1)} custom-call(bf16[128,512]{1,0:T(8,128)(2,1)S(1)} %get-tuple-element.25.act_ref, bf16[3,3,3,32,64]{4,3,2,1,0:T(8,128)(2,1)S(1)} %bitcast.83), custom_call_target="tpu_custom_call" | custom-call | flops 150994944 | bytes 274432 | tf_op jit(solution)/shard_map/pallas_call | solution.py:243
  39.6 0.1 copy.12
  39.9 0.7 %copy.14 = bf16[1,64,4,64]{3,2,1,0:T(4,128)(2,1)} copy(bf16[1,64,4,64]{1,3,2,0:T(8,128)(2,1)S(1)} %bitcast.86) | data formatting | bytes 65536
  40.6 6.4 %all-to-all-done.1 = bf16[32,9,2,128]{3,2,1,0:T(2,128)(2,1)S(1)} async-done(((bf16[32,9,2,128]{3,2,1,0:T(2,128)(2,1)}), bf16[32,9,2,128]{3,2,1,0:T(2,128)(2,1)S(1)}, u32[]{:S(2)}, u32[]{:S(2)}) %all-to-all-start.1) | async-done | bytes 147488 | tf_op jit(solution)/shard_map/all_to_all | solution.py:334
  47.0 1.0 %shard_map.72 = (f32[3,3,3,16,32]{4,3,2,1,0:T(8,128)}, f32[3,3,3,32,64]{4,3,2,1,0:T(8,128)}) custom-call(bf16[576,128]{1,0:T(8,128)(2,1)S(1)} %bitcast.71), custom_call_target="tpu_custom_call" | custom-call | tf_op jit(solution)/shard_map/pallas_call | solution.py:336
  (15 shorter events, 0.5 us)
Async XLA Ops:
  0.6 15.0 %copy-start.2 = (bf16[1,64,4,64]{3,2,1,0:T(4,128)(2,1)S(1)}, bf16[1,64,4,64]{3,2,1,0:T(4,128)(2,1)}, u32[]{:S(2)}) copy-start(bf16[1,64,4,64]{3,2,1,0:T(4,128)(2,1)} %param.7) | copy-start | bytes 98308
  0.6 15.4 %copy-start = (bf16[64,32,3,3,3]{0,1,4,3,2:T(8,128)(2,1)S(1)}, bf16[64,32,3,3,3]{0,1,4,3,2:T(8,128)(2,1)}, u32[]{:S(2)}) copy-start(bf16[64,32,3,3,3]{0,1,4,3,2:T(8,128)(2,1)} %param.6) | copy-start | bytes 331780
  0.7 15.4 %copy-start.1 = (bf16[32,16,3,3,3]{0,1,4,3,2:T(8,128)(2,1)S(1)}, bf16[32,16,3,3,3]{0,1,4,3,2:T(8,128)(2,1)}, u32[]{:S(2)}) copy-start(bf16[32,16,3,3,3]{0,1,4,3,2:T(8,128)(2,1)} %param.5) | copy-start | bytes 82948
  1.9 11.8 %collective-permute-start = (bf16[16,2,1024]{2,1,0:T(2,128)(2,1)S(1)}, bf16[16,2,1024]{2,1,0:T(2,128)(2,1)S(1)}, u32[]{:S(2)}, u32[]{:S(2)}) collective-permute-start(bf16[16,2,1024]{2,1,0:T(2,128)(2,1)S(1)} %get-tuple-element.16), channel_id=1, source_target_pairs={{0,28},{4,24},{8,20},{12,16},{16,12},{20,8},{24,4},{28,0},{1,29},{... | collective-permute-start | bytes 196616 | tf_op jit(solution)/shard_map/ppermute | solution.py:300
  7.9 7.1 %collective-permute-start.1 = (bf16[16,2,1024]{2,1,0:T(2,128)(2,1)S(1)}, bf16[16,2,1024]{2,1,0:T(2,128)(2,1)S(1)}, u32[]{:S(2)}, u32[]{:S(2)}) collective-permute-start(bf16[16,2,1024]{2,1,0:T(2,128)(2,1)S(1)} %get-tuple-element.17), channel_id=1, source_target_pairs={{0,4},{4,0},{8,12},{12,8},{16,20},{20,16},{24,28},{28,24},{1,5},{5... | collective-permute-start | bytes 196616 | tf_op jit(solution)/shard_map/ppermute | solution.py:300
  8.5 8.9 %collective-permute-start.2 = (bf16[16,2,1024]{2,1,0:T(2,128)(2,1)S(1)}, bf16[16,2,1024]{2,1,0:T(2,128)(2,1)S(1)}, u32[]{:S(2)}, u32[]{:S(2)}) collective-permute-start(bf16[16,2,1024]{2,1,0:T(2,128)(2,1)S(1)} %get-tuple-element.18), channel_id=1, source_target_pairs={{0,24},{4,28},{8,16},{12,20},{16,8},{20,12},{24,0},{28,4},{1,25},{... | collective-permute-start | bytes 196616 | tf_op jit(solution)/shard_map/ppermute | solution.py:300
  8.6 9.7 %collective-permute-start.3 = (bf16[16,2,1024]{2,1,0:T(2,128)(2,1)S(1)}, bf16[16,2,1024]{2,1,0:T(2,128)(2,1)S(1)}, u32[]{:S(2)}, u32[]{:S(2)}) collective-permute-start(bf16[16,2,1024]{2,1,0:T(2,128)(2,1)S(1)} %get-tuple-element.19), channel_id=1, source_target_pairs={{0,20},{4,16},{8,28},{12,24},{16,4},{20,0},{24,12},{28,8},{1,21},{... | collective-permute-start | bytes 196616 | tf_op jit(solution)/shard_map/ppermute | solution.py:300
  11.5 7.1 %collective-permute-start.4 = (bf16[16,2,1024]{2,1,0:T(2,128)(2,1)S(1)}, bf16[16,2,1024]{2,1,0:T(2,128)(2,1)S(1)}, u32[]{:S(2)}, u32[]{:S(2)}) collective-permute-start(bf16[16,2,1024]{2,1,0:T(2,128)(2,1)S(1)} %get-tuple-element.34), channel_id=1, source_target_pairs={{0,16},{4,20},{8,24},{12,28},{16,0},{20,4},{24,8},{28,12},{1,17},{... | collective-permute-start | bytes 196616 | tf_op jit(solution)/shard_map/ppermute | solution.py:300
  13.7 6.3 %collective-permute-start.6 = (bf16[16,2,1024]{2,1,0:T(2,128)(2,1)S(1)}, bf16[16,2,1024]{2,1,0:T(2,128)(2,1)S(1)}, u32[]{:S(2)}, u32[]{:S(2)}) collective-permute-start(bf16[16,2,1024]{2,1,0:T(2,128)(2,1)S(1)} %get-tuple-element.32), channel_id=1, source_target_pairs={{0,12},{4,8},{8,4},{12,0},{16,28},{20,24},{24,20},{28,16},{1,13},{... | collective-permute-start | bytes 196616 | tf_op jit(solution)/shard_map/ppermute | solution.py:300
  15.0 5.2 %collective-permute-start.5 = (bf16[16,2,1024]{2,1,0:T(2,128)(2,1)S(1)}, bf16[16,2,1024]{2,1,0:T(2,128)(2,1)S(1)}, u32[]{:S(2)}, u32[]{:S(2)}) collective-permute-start(bf16[16,2,1024]{2,1,0:T(2,128)(2,1)S(1)} %get-tuple-element.33), channel_id=1, source_target_pairs={{0,8},{4,12},{8,0},{12,4},{16,24},{20,28},{24,16},{28,20},{1,9},{5... | collective-permute-start | bytes 196616 | tf_op jit(solution)/shard_map/ppermute | solution.py:300
  36.0 11.0 %all-to-all-start.1 = ((bf16[32,9,2,128]{3,2,1,0:T(2,128)(2,1)}), bf16[32,9,2,128]{3,2,1,0:T(2,128)(2,1)S(1)}, u32[]{:S(2)}, u32[]{:S(2)}) async-start(bf16[32,9,2,128]{3,2,1,0:T(2,128)(2,1)} %bitcast.39), calls=%async_computation.1 | async-start | bytes 294912 | tf_op jit(solution)/shard_map/all_to_all | solution.py:334
where the time goes:
time: 48.3 us; the launch traced here: 48 us
  starting transfers between devices  15.2 us (31%)
  blocking collectives  13.4 us (28%)
  waiting for transfers between devices  8.95 us (19%)
  Pallas kernels  5.99 us (12%)
  local copies, waits for them, and re-layouts  3.67 us (8%)
  between operations  0.8 us (2%)
    all_to_all x1, blocking collectives, body(): mine = lax.all_to_all(blocks, axes, split_axis=0, concat_axis=0, tiled=True)  13.4 us
    ppermute x7, starting transfers between devices, body(): lax.ppermute(block, 'space', [(source, source ^ step) for source in range...  12.6 us
    all_to_all x1, waiting for transfers between devices, body(): lax.all_to_all(spread, axes, split_axis=0, concat_axis=0, tiled=True)  6.43 us
    pallas_call x5, Pallas kernels, call(): pl.pallas_call(kernel, out_shape=tuple(outs), in_specs=[scalar if a.dtype...  5.04 us
    all_to_all x1, starting transfers between devices, body(): lax.all_to_all(spread, axes, split_axis=0, concat_axis=0, tiled=True)  2.58 us
    ppermute x7, waiting for transfers between devices, body(): lax.ppermute(block, 'space', [(source, source ^ step) for source in range...  2.52 us
    squeeze x1, local copies, waits for them, and re-layouts, body(): lax.dynamic_index_in_dim(crops, position ^ step, 0, keepdims=False)  1.21 us
    squeeze x1, local copies, waits for them, and re-layouts, body(): block = lax.dynamic_index_in_dim(rest, position ^ step, 0, keepdims=False)  1.12 us
  transfers between devices with their start and end apart: 8, of which 5 were waited for; matrix products, arithmetic and copies ran while one was open for 5% of the time, Pallas kernels for 6%

commit v1 on v0

--- a/solution.py
+++ b/solution.py
@@ -107,18 +107,21 @@
             out_ref[aw * 256:(aw + 1) * 256, place * 128:(place + 1) * 128] = y[:, aw * 128:(aw + 1) * 128]
 
 
-def layer_kernel(pairs, y_ref, first_ref, second_ref, pick_ref, k1t_ref, ogt_ref, ag_ref, act_ref, terms_ref, y_scr, pg_scr):
+def layer_kernel(first, last, given, y_ref, *refs):
+    pick_ref, k1t_ref, ogt_ref, ag_ref, act_ref, terms_ref, y_scr, pg_scr = refs[len(given):]
     cells = ag_ref.shape[1]
     rows = 256
     here = lax.axis_index("space") >> 1
-    for place, m in enumerate(pairs):
-        lanes = pl.ds(pl.multiple_of(lax.bitwise_xor(here, jnp.int32(m)) * 128, 128), 128)
-        if place + 1 < len(pairs):
-            y_scr[:, lanes] = y_ref[:, place * 128:(place + 1) * 128]
-            continue
-        y = taps_of_pair(first_ref, second_ref, pick_ref)
-        for aw in range(3):
-            y_scr[aw * rows:(aw + 1) * rows, lanes] = y[:, aw * 128:(aw + 1) * 128]
+
+    def lanes(m):
+        return pl.ds(pl.multiple_of(lax.bitwise_xor(here, jnp.int32(m)) * 128, 128), 128)
+
+    for place, m in enumerate(first):
+        y_scr[:, lanes(m)] = y_ref[:, place * 128:(place + 1) * 128]
+    for m in last:
+        y = taps_of_pair(refs[given.index(2 * m)], refs[given.index(2 * m + 1)], pick_ref)
+        for aw in range(3):
+            y_scr[aw * rows:(aw + 1) * rows, lanes(m)] = y[:, aw * 128:(aw + 1) * 128]
     both = dot(k1t_ref[...], y_scr[...])
     lane = iota((128, cells), 1)
     from_last = jnp.where(lane < 64, 0.0, pltpu.roll(both[128:], 64, 1))
@@ -282,11 +285,11 @@
     space = lax.axis_size("space")
     assert space & (space - 1) == 0
     position = lax.axis_index("space").astype(jnp.int32)
-    across = list(range(space - 1, space // 2 - 1, -1))
-    order = across[:1] + [1] + across[1:] + list(range(4, space // 2)) + [2, 3]
+    across, near = range(space - 1, space // 2 - 1, -1), range(1, space // 2)
+    order = [step for two in zip(across, near) for step in two] + [space // 2]
     early, late = order[:space // 2], order[space // 2:]
-    last = 1
-    pairs = [m for m in range(space // 2) if m != last] + [last]
+    last = sorted({step // 2 for step in order[-3:]})
+    first = [m for m in range(space // 2) if m not in last]
     k1, k2 = by_tap(first_kernel), by_tap(second_kernel)
     x = {}
     cut = [lax.dynamic_index_in_dim(crops, position ^ step, 0, keepdims=False) for step in early]
@@ -303,18 +306,19 @@
         x[step] = block.reshape(channels_in * two * HEIGHT, WIDTH)
     pick, k1t, ogt, act_grad = prepare(k1, k2, out_grad)
     cells = act_grad.shape[1]
-    given = early + [step for step in x if step not in early and step // 2 != last]
+    given = [step for step in order + [0] if step // 2 in first]
     (y,) = call(
-        functools.partial(taps_kernel, pairs[:-1], given),
-        [array((768, cells - 128))],
+        functools.partial(taps_kernel, first, given),
+        [array((768, len(first) * 128))],
         [x[step] for step in given] + [pick],
         flops=2 * 256 * 384 * cells,
     )
+    given = [step for step in order[::-1] if step // 2 in last]
     rows = -(-TERM_ROWS // (devices * 2)) * 2
     act, terms = call(
-        functools.partial(layer_kernel, pairs),
+        functools.partial(layer_kernel, first, last, given),
         [array((128, cells)), array((devices * rows, LANES))],
-        (y, x[2 * last], x[2 * last + 1], pick, k1t, ogt, act_grad),
+        (y, *[x[step] for step in given], pick, k1t, ogt, act_grad),
         scratch=[pltpu.VMEM((768, cells), jnp.bfloat16), pltpu.VMEM((256, cells), jnp.bfloat16)],
         flops=2 * 128 * 4096 * cells,
     )

time: 48.3 us -> 47.5 us (0.983)
  blocking collectives: 13.4 us -> 12.5 us
  waiting for transfers between devices: 8.95 us -> 8.42 us
  starting transfers between devices: 15.2 us -> 15.7 us
    all_to_all x1, blocking collectives: 13.4 us -> 12.5 us  [body(): mine = lax.all_to_all(blocks, axes, split_axis=0, concat_axis=0, tiled=True)]
    ppermute x7, starting transfers between devices: 12.6 us -> 13.2 us  [body(): lax.ppermute(block, 'space', [(source, source ^ step) for source in range...]
    ppermute x7, waiting for transfers between devices: 2.52 us -> 2 us  [body(): lax.ppermute(block, 'space', [(source, source ^ step) for source in range...]
  transfers between devices with their start and end apart: 8 -> 8, of which waited for: 5 -> 3; matrix products, arithmetic and copies ran while one was open for 5% -> 5% of each run, Pallas kernels for 6% -> 5%
where the time goes in v1:
time: 47.5 us; the launch traced here: 47.2 us
  starting transfers between devices  15.7 us (33%)
  blocking collectives  12.5 us (26%)
  waiting for transfers between devices  8.42 us (18%)
  Pallas kernels  6.01 us (13%)
  local copies, waits for them, and re-layouts  3.67 us (8%)
  between operations  0.81 us (2%)
    ppermute x7, starting transfers between devices, body(): lax.ppermute(block, 'space', [(source, source ^ step) for source in range...  13.2 us
    all_to_all x1, blocking collectives, body(): mine = lax.all_to_all(blocks, axes, split_axis=0, concat_axis=0, tiled=True)  12.5 us
    all_to_all x1, waiting for transfers between devices, body(): lax.all_to_all(spread, axes, split_axis=0, concat_axis=0, tiled=True)  6.43 us
    pallas_call x5, Pallas kernels, call(): pl.pallas_call(kernel, out_shape=tuple(outs), in_specs=[scalar if a.dtype...  5.05 us
    all_to_all x1, starting transfers between devices, body(): lax.all_to_all(spread, axes, split_axis=0, concat_axis=0, tiled=True)  2.58 us
    ppermute x7, waiting for transfers between devices, body(): lax.ppermute(block, 'space', [(source, source ^ step) for source in range...  2 us
    squeeze x1, local copies, waits for them, and re-layouts, body(): lax.dynamic_index_in_dim(crops, position ^ step, 0, keepdims=False)  1.21 us
    squeeze x1, local copies, waits for them, and re-layouts, body(): block = lax.dynamic_index_in_dim(rest, position ^ step, 0, keepdims=False)  1.12 us
  transfers between devices with their start and end apart: 8, of which 3 were waited for; matrix products, arithmetic and copies ran while one was open for 5% of the time, Pallas kernels for 5%

profile of v1, /device:TPU:0, one launch (start us, length us, event | category | flops | bytes accessed | tf_op | source)
XLA Modules:
  0.0 47.2 jit_solution(5010267765210133087)
XLA Ops:
  0.7 1.2 %dynamic-slice_bitcast_fusion.3 = (bf16[16,2,1024]{2,1,0:T(2,128)(2,1)S(1)}, bf16[16,2,1024]{2,1,0:T(2,128)(2,1)S(1)}, bf16[16,2,1024]{2,1,0:T(2,128)(2,1)S(1)}, bf16[16,2,1024]{2,1,0:T(2,128)(2,1)S(1)}) fusion(bf16[8,16,2,1024]{3,2,1,0:T(2,128)(2,1)} %param.4, s32[]{:T(128)S(6)} %select_n.28, s32[]{:T(128)S(6)} %select_n.27, s32[]{:T(128)S(6)} %select_n.26, ...), kind=kLoop, calls=%fused_computation.3 | loop fusion | bytes 524304 | tf_op jit(solution)/shard_map/jit(dynamic_index_in_dim)/squeeze | solution.py:295
  1.9 6.0 %collective-permute-start = (bf16[16,2,1024]{2,1,0:T(2,128)(2,1)S(1)}, bf16[16,2,1024]{2,1,0:T(2,128)(2,1)S(1)}, u32[]{:S(2)}, u32[]{:S(2)}) collective-permute-start(bf16[16,2,1024]{2,1,0:T(2,128)(2,1)S(1)} %get-tuple-element.16), channel_id=1, source_target_pairs={{0,28},{4,24},{8,20},{12,16},{16,12},{20,8},{24,4},{28,0},{1,29},{... | collective-permute-start | bytes 196616 | tf_op jit(solution)/shard_map/ppermute | solution.py:303
  7.9 0.5 %collective-permute-start.1 = (bf16[16,2,1024]{2,1,0:T(2,128)(2,1)S(1)}, bf16[16,2,1024]{2,1,0:T(2,128)(2,1)S(1)}, u32[]{:S(2)}, u32[]{:S(2)}) collective-permute-start(bf16[16,2,1024]{2,1,0:T(2,128)(2,1)S(1)} %get-tuple-element.17), channel_id=1, source_target_pairs={{0,4},{4,0},{8,12},{12,8},{16,20},{20,16},{24,28},{28,24},{1,5},{5... | collective-permute-start | bytes 196616 | tf_op jit(solution)/shard_map/ppermute | solution.py:303
  8.5 0.1 collective-permute-start.2
  8.6 1.1 %dynamic-slice_bitcast_fusion = (bf16[16,2,1024]{2,1,0:T(2,128)(2,1)S(1)}, bf16[16,2,1024]{2,1,0:T(2,128)(2,1)S(1)}, bf16[16,2,1024]{2,1,0:T(2,128)(2,1)S(1)}, bf16[1,16,2,1024]{3,2,1,0:T(2,128)(2,1)S(1)}) fusion(bf16[8,16,2,1024]{3,2,1,0:T(2,128)(2,1)} %param.4, s32[]{:T(128)S(6)} %select_n.32, s32[]{:T(128)S(6)} %select_n.31, s32[]{:T(128)S(6)} %select_n.30, ...), kind=kLoop, calls=%fused_computation | loop fusion | bytes 524304 | tf_op jit(solution)/shard_map/jit(dynamic_index_in_dim)/squeeze | solution.py:301
  9.7 5.3 %collective-permute-start.5 = (bf16[16,2,1024]{2,1,0:T(2,128)(2,1)S(1)}, bf16[16,2,1024]{2,1,0:T(2,128)(2,1)S(1)}, u32[]{:S(2)}, u32[]{:S(2)}) collective-permute-start(bf16[16,2,1024]{2,1,0:T(2,128)(2,1)S(1)} %get-tuple-element.32), channel_id=1, source_target_pairs={{0,20},{4,16},{8,28},{12,24},{16,4},{20,0},{24,12},{28,8},{1,21},{... | collective-permute-start | bytes 196616 | tf_op jit(solution)/shard_map/ppermute | solution.py:303
  15.0 1.2 %collective-permute-start.3 = (bf16[16,2,1024]{2,1,0:T(2,128)(2,1)S(1)}, bf16[16,2,1024]{2,1,0:T(2,128)(2,1)S(1)}, u32[]{:S(2)}, u32[]{:S(2)}) collective-permute-start(bf16[16,2,1024]{2,1,0:T(2,128)(2,1)S(1)} %get-tuple-element.34), channel_id=1, source_target_pairs={{0,16},{4,20},{8,24},{12,28},{16,0},{20,4},{24,8},{28,12},{1,17},{... | collective-permute-start | bytes 196616 | tf_op jit(solution)/shard_map/ppermute | solution.py:303
  16.2 0.1 copy.9
  16.4 0.1 reshape.88
  16.5 0.1 copy.11.og_ref
  16.6 1.3 %shard_map.67 = (bf16[384,384]{1,0:T(8,128)(2,1)S(1)}, bf16[256,768]{1,0:T(8,128)(2,1)S(1)}, bf16[512,1152]{1,0:T(8,128)(2,1)S(1)}, bf16[128,512]{1,0:T(8,128)(2,1)S(1)}) custom-call(bf16[3,3,3,16,32]{4,3,2,1,0:T(8,128)(2,1)S(1)} %bitcast.84, bf16[3,3,3,32,64]{4,3,2,1,0:T(8,128)(2,1)S(1)} %bitcast.82, bf16[128,128]{1,0:T(8,128)(2,1)S(1)} %copy.11.og_ref), custom_call_target="tpu_custom_call" | custom-call | flops 301989888 | bytes 2169856 | tf_op jit(solution)/shard_map/pallas_call | solution.py:246
  17.9 0.3 shard_map.68.y_ref
  18.2 1.9 %collective-permute-done.4 = bf16[16,2,1024]{2,1,0:T(2,128)(2,1)S(1)} collective-permute-done((bf16[16,2,1024]{2,1,0:T(2,128)(2,1)S(1)}, bf16[16,2,1024]{2,1,0:T(2,128)(2,1)S(1)}, u32[]{:S(2)}, u32[]{:S(2)}) %collective-permute-start.4) | collective-permute-done | bytes 65568 | tf_op jit(solution)/shard_map/ppermute | solution.py:303
  20.1 0.1 collective-permute-done.3
  20.2 1.8 %shard_map.69 = (bf16[128,512]{1,0:T(8,128)(2,1)S(1)}, bf16[576,128]{1,0:T(8,128)(2,1)S(1)}) custom-call(bf16[768,256]{1,0:T(8,128)(2,1)S(1)} %shard_map.68.y_ref, bf16[256,128]{1,0:T(8,128)(2,1)S(1)} %bitcast.81, bf16[256,128]{1,0:T(8,128)(2,1)S(1)} %bitcast.80, bf16[256,128]{1,0:T(8,128)(2,1)S(1)} %bitcast.79, bf16[256,128]{1,0:T(8,128)(2,1)S(1)} %bitcast.78, ...), custom_call_target="tpu_custom_call" | custom-call | flops 536870912 | bytes 2932736 | tf_op jit(solution)/shard_map/pallas_call | solution.py:246
  22.0 12.5 %all_to_all.10 = bf16[32,9,2,128]{3,2,1,0:T(2,128)(2,1)S(1)} all-to-all(bf16[32,9,2,128]{3,2,1,0:T(2,128)(2,1)S(1)} %bitcast.74), channel_id=1, replica_groups=mesh['space'=8,'sample'=4] {'space','sample'}, dimensions={0} | all-to-all | bytes 294912 | tf_op jit(solution)/shard_map/all_to_all | solution.py:326
  34.5 0.7 %shard_map.71 = bf16[576,128]{1,0:T(8,128)(2,1)} custom-call(bf16[576,128]{1,0:T(8,128)(2,1)S(1)} %bitcast.72), custom_call_target="tpu_custom_call" | custom-call | bytes 294912 | tf_op jit(solution)/shard_map/pallas_call | solution.py:246
  35.2 2.6 %all-to-all-start.1 = ((bf16[32,9,2,128]{3,2,1,0:T(2,128)(2,1)}), bf16[32,9,2,128]{3,2,1,0:T(2,128)(2,1)S(1)}, u32[]{:S(2)}, u32[]{:S(2)}) async-start(bf16[32,9,2,128]{3,2,1,0:T(2,128)(2,1)} %bitcast.39), calls=%async_computation.1 | async-start | bytes 294912 | tf_op jit(solution)/shard_map/all_to_all | solution.py:338
  37.8 1.0 %shard_map.70 = bf16[128,128]{1,0:T(8,128)(2,1)S(1)} custom-call(bf16[128,512]{1,0:T(8,128)(2,1)S(1)} %get-tuple-element.25.act_ref, bf16[3,3,3,32,64]{4,3,2,1,0:T(8,128)(2,1)S(1)} %bitcast.83), custom_call_target="tpu_custom_call" | custom-call | flops 150994944 | bytes 274432 | tf_op jit(solution)/shard_map/pallas_call | solution.py:246
  38.8 0.1 copy.12
  38.9 0.1 reshape.97
  39.1 0.7 %copy.14 = bf16[1,64,4,64]{3,2,1,0:T(4,128)(2,1)} copy(bf16[1,64,4,64]{1,3,2,0:T(8,128)(2,1)S(1)} %bitcast.86) | data formatting | bytes 65536
  39.8 6.4 %all-to-all-done.1 = bf16[32,9,2,128]{3,2,1,0:T(2,128)(2,1)S(1)} async-done(((bf16[32,9,2,128]{3,2,1,0:T(2,128)(2,1)}), bf16[32,9,2,128]{3,2,1,0:T(2,128)(2,1)S(1)}, u32[]{:S(2)}, u32[]{:S(2)}) %all-to-all-start.1) | async-done | bytes 147488 | tf_op jit(solution)/shard_map/all_to_all | solution.py:338
  46.2 1.0 %shard_map.72 = (f32[3,3,3,16,32]{4,3,2,1,0:T(8,128)}, f32[3,3,3,32,64]{4,3,2,1,0:T(8,128)}) custom-call(bf16[576,128]{1,0:T(8,128)(2,1)S(1)} %bitcast.71), custom_call_target="tpu_custom_call" | custom-call | tf_op jit(solution)/shard_map/pallas_call | solution.py:340
  (15 shorter events, 0.1 us)
Async XLA Ops:
  0.6 15.6 %copy-start.2 = (bf16[1,64,4,64]{3,2,1,0:T(4,128)(2,1)S(1)}, bf16[1,64,4,64]{3,2,1,0:T(4,128)(2,1)}, u32[]{:S(2)}) copy-start(bf16[1,64,4,64]{3,2,1,0:T(4,128)(2,1)} %param.7) | copy-start | bytes 98308
  0.6 15.9 %copy-start = (bf16[64,32,3,3,3]{0,1,4,3,2:T(8,128)(2,1)S(1)}, bf16[64,32,3,3,3]{0,1,4,3,2:T(8,128)(2,1)}, u32[]{:S(2)}) copy-start(bf16[64,32,3,3,3]{0,1,4,3,2:T(8,128)(2,1)} %param.6) | copy-start | bytes 331780
  0.7 15.9 %copy-start.1 = (bf16[32,16,3,3,3]{0,1,4,3,2:T(8,128)(2,1)S(1)}, bf16[32,16,3,3,3]{0,1,4,3,2:T(8,128)(2,1)}, u32[]{:S(2)}) copy-start(bf16[32,16,3,3,3]{0,1,4,3,2:T(8,128)(2,1)} %param.5) | copy-start | bytes 82948
  1.9 13.1 %collective-permute-start = (bf16[16,2,1024]{2,1,0:T(2,128)(2,1)S(1)}, bf16[16,2,1024]{2,1,0:T(2,128)(2,1)S(1)}, u32[]{:S(2)}, u32[]{:S(2)}) collective-permute-start(bf16[16,2,1024]{2,1,0:T(2,128)(2,1)S(1)} %get-tuple-element.16), channel_id=1, source_target_pairs={{0,28},{4,24},{8,20},{12,16},{16,12},{20,8},{24,4},{28,0},{1,29},{... | collective-permute-start | bytes 196616 | tf_op jit(solution)/shard_map/ppermute | solution.py:303
  7.9 7.0 %collective-permute-start.1 = (bf16[16,2,1024]{2,1,0:T(2,128)(2,1)S(1)}, bf16[16,2,1024]{2,1,0:T(2,128)(2,1)S(1)}, u32[]{:S(2)}, u32[]{:S(2)}) collective-permute-start(bf16[16,2,1024]{2,1,0:T(2,128)(2,1)S(1)} %get-tuple-element.17), channel_id=1, source_target_pairs={{0,4},{4,0},{8,12},{12,8},{16,20},{20,16},{24,28},{28,24},{1,5},{5... | collective-permute-start | bytes 196616 | tf_op jit(solution)/shard_map/ppermute | solution.py:303
  8.5 9.4 %collective-permute-start.2 = (bf16[16,2,1024]{2,1,0:T(2,128)(2,1)S(1)}, bf16[16,2,1024]{2,1,0:T(2,128)(2,1)S(1)}, u32[]{:S(2)}, u32[]{:S(2)}) collective-permute-start(bf16[16,2,1024]{2,1,0:T(2,128)(2,1)S(1)} %get-tuple-element.18), channel_id=1, source_target_pairs={{0,24},{4,28},{8,16},{12,20},{16,8},{20,12},{24,0},{28,4},{1,25},{... | collective-permute-start | bytes 196616 | tf_op jit(solution)/shard_map/ppermute | solution.py:303
  8.6 9.6 %collective-permute-start.6 = (bf16[16,2,1024]{2,1,0:T(2,128)(2,1)S(1)}, bf16[16,2,1024]{2,1,0:T(2,128)(2,1)S(1)}, u32[]{:S(2)}, u32[]{:S(2)}) collective-permute-start(bf16[16,2,1024]{2,1,0:T(2,128)(2,1)S(1)} %get-tuple-element.21), channel_id=1, source_target_pairs={{0,8},{4,12},{8,0},{12,4},{16,24},{20,28},{24,16},{28,20},{1,9},{5... | collective-permute-start | bytes 196616 | tf_op jit(solution)/shard_map/ppermute | solution.py:303
  9.7 8.5 %collective-permute-start.5 = (bf16[16,2,1024]{2,1,0:T(2,128)(2,1)S(1)}, bf16[16,2,1024]{2,1,0:T(2,128)(2,1)S(1)}, u32[]{:S(2)}, u32[]{:S(2)}) collective-permute-start(bf16[16,2,1024]{2,1,0:T(2,128)(2,1)S(1)} %get-tuple-element.32), channel_id=1, source_target_pairs={{0,20},{4,16},{8,28},{12,24},{16,4},{20,0},{24,12},{28,8},{1,21},{... | collective-permute-start | bytes 196616 | tf_op jit(solution)/shard_map/ppermute | solution.py:303
  15.0 5.2 %collective-permute-start.4 = (bf16[16,2,1024]{2,1,0:T(2,128)(2,1)S(1)}, bf16[16,2,1024]{2,1,0:T(2,128)(2,1)S(1)}, u32[]{:S(2)}, u32[]{:S(2)}) collective-permute-start(bf16[16,2,1024]{2,1,0:T(2,128)(2,1)S(1)} %get-tuple-element.33), channel_id=1, source_target_pairs={{0,12},{4,8},{8,4},{12,0},{16,28},{20,24},{24,20},{28,16},{1,13},{... | collective-permute-start | bytes 196616 | tf_op jit(solution)/shard_map/ppermute | solution.py:303
  15.0 5.2 %collective-permute-start.3 = (bf16[16,2,1024]{2,1,0:T(2,128)(2,1)S(1)}, bf16[16,2,1024]{2,1,0:T(2,128)(2,1)S(1)}, u32[]{:S(2)}, u32[]{:S(2)}) collective-permute-start(bf16[16,2,1024]{2,1,0:T(2,128)(2,1)S(1)} %get-tuple-element.34), channel_id=1, source_target_pairs={{0,16},{4,20},{8,24},{12,28},{16,0},{20,4},{24,8},{28,12},{1,17},{... | collective-permute-start | bytes 196616 | tf_op jit(solution)/shard_map/ppermute | solution.py:303
  35.2 11.0 %all-to-all-start.1 = ((bf16[32,9,2,128]{3,2,1,0:T(2,128)(2,1)}), bf16[32,9,2,128]{3,2,1,0:T(2,128)(2,1)S(1)}, u32[]{:S(2)}, u32[]{:S(2)}) async-start(bf16[32,9,2,128]{3,2,1,0:T(2,128)(2,1)} %bitcast.39), calls=%async_computation.1 | async-start | bytes 294912 | tf_op jit(solution)/shard_map/all_to_all | solution.py:338

commit v2 on v1

--- a/solution.py
+++ b/solution.py
@@ -287,7 +287,7 @@
     position = lax.axis_index("space").astype(jnp.int32)
     across, near = range(space - 1, space // 2 - 1, -1), range(1, space // 2)
     order = [step for two in zip(across, near) for step in two] + [space // 2]
-    early, late = order[:space // 2], order[space // 2:]
+    early, late = order[:2], order[2:]
     last = sorted({step // 2 for step in order[-3:]})
     first = [m for m in range(space // 2) if m not in last]
     k1, k2 = by_tap(first_kernel), by_tap(second_kernel)

time: 47.5 us -> 47.4 us (level)
  waiting for transfers between devices: 8.42 us -> 9 us
  starting transfers between devices: 15.7 us -> 15.2 us
    ppermute x7, waiting for transfers between devices: 2 us -> 2.57 us  [body(): lax.ppermute(block, 'space', [(source, source ^ step) for source in range...]
    ppermute x7, starting transfers between devices: 13.2 us -> 12.6 us  [body(): lax.ppermute(block, 'space', [(source, source ^ step) for source in range...]
  transfers between devices with their start and end apart: 8 -> 8, of which waited for: 3 -> 4; matrix products, arithmetic and copies ran while one was open for 5% -> 6% of each run, Pallas kernels for 5% -> 5%
where the time goes in v2:
time: 47.4 us; the launch traced here: 47.2 us
  starting transfers between devices  15.2 us (32%)
  blocking collectives  12.5 us (26%)
  waiting for transfers between devices  9 us (19%)
  Pallas kernels  6.01 us (13%)
  local copies, waits for them, and re-layouts  3.65 us (8%)
  between operations  0.8 us (2%)
    ppermute x7, starting transfers between devices, body(): lax.ppermute(block, 'space', [(source, source ^ step) for source in range...  12.6 us
    all_to_all x1, blocking collectives, body(): mine = lax.all_to_all(blocks, axes, split_axis=0, concat_axis=0, tiled=True)  12.5 us
    all_to_all x1, waiting for transfers between devices, body(): lax.all_to_all(spread, axes, split_axis=0, concat_axis=0, tiled=True)  6.43 us
    pallas_call x5, Pallas kernels, call(): pl.pallas_call(kernel, out_shape=tuple(outs), in_specs=[scalar if a.dtype...  5.05 us
    all_to_all x1, starting transfers between devices, body(): lax.all_to_all(spread, axes, split_axis=0, concat_axis=0, tiled=True)  2.58 us
    ppermute x7, waiting for transfers between devices, body(): lax.ppermute(block, 'space', [(source, source ^ step) for source in range...  2.57 us
    squeeze x1, local copies, waits for them, and re-layouts, body(): block = lax.dynamic_index_in_dim(rest, position ^ step, 0, keepdims=False)  1.27 us
    squeeze x1, local copies, waits for them, and re-layouts, body(): lax.dynamic_index_in_dim(crops, position ^ step, 0, keepdims=False)  1.04 us
  transfers between devices with their start and end apart: 8, of which 4 were waited for; matrix products, arithmetic and copies ran while one was open for 6% of the time, Pallas kernels for 5%

profile of v2, /device:TPU:0, one launch (start us, length us, event | category | flops | bytes accessed | tf_op | source)
XLA Modules:
  0.0 47.2 jit_solution(5169754257027075458)
XLA Ops:
  0.7 1.0 %dynamic-slice_bitcast_fusion.5 = (bf16[16,2,1024]{2,1,0:T(2,128)(2,1)S(1)}, bf16[16,2,1024]{2,1,0:T(2,128)(2,1)S(1)}) fusion(bf16[8,16,2,1024]{3,2,1,0:T(2,128)(2,1)} %param.4, s32[]{:T(128)S(6)} %select_n.26, s32[]{:T(128)S(6)} %select_n.25), kind=kLoop, calls=%fused_computation.5 | loop fusion | bytes 262152 | tf_op jit(solution)/shard_map/jit(dynamic_index_in_dim)/squeeze | solution.py:295
  1.7 6.0 %collective-permute-start = (bf16[16,2,1024]{2,1,0:T(2,128)(2,1)S(1)}, bf16[16,2,1024]{2,1,0:T(2,128)(2,1)S(1)}, u32[]{:S(2)}, u32[]{:S(2)}) collective-permute-start(bf16[16,2,1024]{2,1,0:T(2,128)(2,1)S(1)} %get-tuple-element.14), channel_id=1, source_target_pairs={{0,28},{4,24},{8,20},{12,16},{16,12},{20,8},{24,4},{28,0},{1,29},{... | collective-permute-start | bytes 196616 | tf_op jit(solution)/shard_map/ppermute | solution.py:303
  7.8 0.5 %collective-permute-start.1 = (bf16[16,2,1024]{2,1,0:T(2,128)(2,1)S(1)}, bf16[16,2,1024]{2,1,0:T(2,128)(2,1)S(1)}, u32[]{:S(2)}, u32[]{:S(2)}) collective-permute-start(bf16[16,2,1024]{2,1,0:T(2,128)(2,1)S(1)} %get-tuple-element.15), channel_id=1, source_target_pairs={{0,4},{4,0},{8,12},{12,8},{16,20},{20,16},{24,28},{28,24},{1,5},{5... | collective-permute-start | bytes 196616 | tf_op jit(solution)/shard_map/ppermute | solution.py:303
  8.3 1.3 %dynamic-slice_bitcast_fusion = (bf16[16,2,1024]{2,1,0:T(2,128)(2,1)S(1)}, bf16[16,2,1024]{2,1,0:T(2,128)(2,1)S(1)}, bf16[16,2,1024]{2,1,0:T(2,128)(2,1)S(1)}, b...) fusion(bf16[8,16,2,1024]{3,2,1,0:T(2,128)(2,1)} %param.4, ...), kind=kLoop, calls=%fused_computation | loop fusion | bytes 786456 | tf_op jit(solution)/shard_map/jit(dynamic_index_in_dim)/squeeze | solution.py:301
  9.6 0.2 collective-permute-start.2
  9.7 5.2 %collective-permute-start.5 = (bf16[16,2,1024]{2,1,0:T(2,128)(2,1)S(1)}, bf16[16,2,1024]{2,1,0:T(2,128)(2,1)S(1)}, u32[]{:S(2)}, u32[]{:S(2)}) collective-permute-start(bf16[16,2,1024]{2,1,0:T(2,128)(2,1)S(1)} %get-tuple-element.29), channel_id=1, source_target_pairs={{0,20},{4,16},{8,28},{12,24},{16,4},{20,0},{24,12},{28,8},{1,21},{... | collective-permute-start | bytes 196616 | tf_op jit(solution)/shard_map/ppermute | solution.py:303
  15.0 0.6 %collective-permute-start.3 = (bf16[16,2,1024]{2,1,0:T(2,128)(2,1)S(1)}, bf16[16,2,1024]{2,1,0:T(2,128)(2,1)S(1)}, u32[]{:S(2)}, u32[]{:S(2)}) collective-permute-start(bf16[16,2,1024]{2,1,0:T(2,128)(2,1)S(1)} %get-tuple-element.31), channel_id=1, source_target_pairs={{0,16},{4,20},{8,24},{12,28},{16,0},{20,4},{24,8},{28,12},{1,17},{... | collective-permute-start | bytes 196616 | tf_op jit(solution)/shard_map/ppermute | solution.py:303
  15.6 0.1 copy.9
  15.8 0.1 reshape.88
  15.9 0.1 copy.11.og_ref
  16.0 1.3 %shard_map.67 = (bf16[384,384]{1,0:T(8,128)(2,1)S(1)}, bf16[256,768]{1,0:T(8,128)(2,1)S(1)}, bf16[512,1152]{1,0:T(8,128)(2,1)S(1)}, bf16[128,512]{1,0:T(8,128)(2,1)S(1)}) custom-call(bf16[3,3,3,16,32]{4,3,2,1,0:T(8,128)(2,1)S(1)} %bitcast.84, bf16[3,3,3,32,64]{4,3,2,1,0:T(8,128)(2,1)S(1)} %bitcast.82, bf16[128,128]{1,0:T(8,128)(2,1)S(1)} %copy.11.og_ref), custom_call_target="tpu_custom_call" | custom-call | flops 301989888 | bytes 2169856 | tf_op jit(solution)/shard_map/pallas_call | solution.py:246
  17.3 0.3 shard_map.68.y_ref
  17.6 0.1 collective-permute-done.5
  17.7 2.4 %collective-permute-done.4 = bf16[16,2,1024]{2,1,0:T(2,128)(2,1)S(1)} collective-permute-done((bf16[16,2,1024]{2,1,0:T(2,128)(2,1)S(1)}, bf16[16,2,1024]{2,1,0:T(2,128)(2,1)S(1)}, u32[]{:S(2)}, u32[]{:S(2)}) %collective-permute-start.4) | collective-permute-done | bytes 65568 | tf_op jit(solution)/shard_map/ppermute | solution.py:303
  20.2 1.8 %shard_map.69 = (bf16[128,512]{1,0:T(8,128)(2,1)S(1)}, bf16[576,128]{1,0:T(8,128)(2,1)S(1)}) custom-call(bf16[768,256]{1,0:T(8,128)(2,1)S(1)} %shard_map.68.y_ref, bf16[256,128]{1,0:T(8,128)(2,1)S(1)} %bitcast.81, bf16[256,128]{1,0:T(8,128)(2,1)S(1)} %bitcast.80, bf16[256,128]{1,0:T(8,128)(2,1)S(1)} %bitcast.79, bf16[256,128]{1,0:T(8,128)(2,1)S(1)} %bitcast.78, ...), custom_call_target="tpu_custom_call" | custom-call | flops 536870912 | bytes 2932736 | tf_op jit(solution)/shard_map/pallas_call | solution.py:246
  22.0 12.5 %all_to_all.10 = bf16[32,9,2,128]{3,2,1,0:T(2,128)(2,1)S(1)} all-to-all(bf16[32,9,2,128]{3,2,1,0:T(2,128)(2,1)S(1)} %bitcast.74), channel_id=1, replica_groups=mesh['space'=8,'sample'=4] {'space','sample'}, dimensions={0} | all-to-all | bytes 294912 | tf_op jit(solution)/shard_map/all_to_all | solution.py:326
  34.5 0.7 %shard_map.71 = bf16[576,128]{1,0:T(8,128)(2,1)} custom-call(bf16[576,128]{1,0:T(8,128)(2,1)S(1)} %bitcast.72), custom_call_target="tpu_custom_call" | custom-call | bytes 294912 | tf_op jit(solution)/shard_map/pallas_call | solution.py:246
  35.2 2.6 %all-to-all-start.1 = ((bf16[32,9,2,128]{3,2,1,0:T(2,128)(2,1)}), bf16[32,9,2,128]{3,2,1,0:T(2,128)(2,1)S(1)}, u32[]{:S(2)}, u32[]{:S(2)}) async-start(bf16[32,9,2,128]{3,2,1,0:T(2,128)(2,1)} %bitcast.39), calls=%async_computation.1 | async-start | bytes 294912 | tf_op jit(solution)/shard_map/all_to_all | solution.py:338
  37.8 1.0 %shard_map.70 = bf16[128,128]{1,0:T(8,128)(2,1)S(1)} custom-call(bf16[128,512]{1,0:T(8,128)(2,1)S(1)} %get-tuple-element.21.act_ref, bf16[3,3,3,32,64]{4,3,2,1,0:T(8,128)(2,1)S(1)} %bitcast.83), custom_call_target="tpu_custom_call" | custom-call | flops 150994944 | bytes 274432 | tf_op jit(solution)/shard_map/pallas_call | solution.py:246
  38.8 0.1 copy.12
  38.9 0.1 reshape.97
  39.0 0.7 %copy.14 = bf16[1,64,4,64]{3,2,1,0:T(4,128)(2,1)} copy(bf16[1,64,4,64]{1,3,2,0:T(8,128)(2,1)S(1)} %bitcast.86) | data formatting | bytes 65536
  39.8 6.4 %all-to-all-done.1 = bf16[32,9,2,128]{3,2,1,0:T(2,128)(2,1)S(1)} async-done(((bf16[32,9,2,128]{3,2,1,0:T(2,128)(2,1)}), bf16[32,9,2,128]{3,2,1,0:T(2,128)(2,1)S(1)}, u32[]{:S(2)}, u32[]{:S(2)}) %all-to-all-start.1) | async-done | bytes 147488 | tf_op jit(solution)/shard_map/all_to_all | solution.py:338
  46.2 1.0 %shard_map.72 = (f32[3,3,3,16,32]{4,3,2,1,0:T(8,128)}, f32[3,3,3,32,64]{4,3,2,1,0:T(8,128)}) custom-call(bf16[576,128]{1,0:T(8,128)(2,1)S(1)} %bitcast.71), custom_call_target="tpu_custom_call" | custom-call | tf_op jit(solution)/shard_map/pallas_call | solution.py:340
  (15 shorter events, 0.2 us)
Async XLA Ops:
  0.6 15.0 %copy-start.2 = (bf16[1,64,4,64]{3,2,1,0:T(4,128)(2,1)S(1)}, bf16[1,64,4,64]{3,2,1,0:T(4,128)(2,1)}, u32[]{:S(2)}) copy-start(bf16[1,64,4,64]{3,2,1,0:T(4,128)(2,1)} %param.7) | copy-start | bytes 98308
  0.6 15.4 %copy-start = (bf16[64,32,3,3,3]{0,1,4,3,2:T(8,128)(2,1)S(1)}, bf16[64,32,3,3,3]{0,1,4,3,2:T(8,128)(2,1)}, u32[]{:S(2)}) copy-start(bf16[64,32,3,3,3]{0,1,4,3,2:T(8,128)(2,1)} %param.6) | copy-start | bytes 331780
  0.7 15.4 %copy-start.1 = (bf16[32,16,3,3,3]{0,1,4,3,2:T(8,128)(2,1)S(1)}, bf16[32,16,3,3,3]{0,1,4,3,2:T(8,128)(2,1)}, u32[]{:S(2)}) copy-start(bf16[32,16,3,3,3]{0,1,4,3,2:T(8,128)(2,1)} %param.5) | copy-start | bytes 82948
  1.7 13.2 %collective-permute-start = (bf16[16,2,1024]{2,1,0:T(2,128)(2,1)S(1)}, bf16[16,2,1024]{2,1,0:T(2,128)(2,1)S(1)}, u32[]{:S(2)}, u32[]{:S(2)}) collective-permute-start(bf16[16,2,1024]{2,1,0:T(2,128)(2,1)S(1)} %get-tuple-element.14), channel_id=1, source_target_pairs={{0,28},{4,24},{8,20},{12,16},{16,12},{20,8},{24,4},{28,0},{1,29},{... | collective-permute-start | bytes 196616 | tf_op jit(solution)/shard_map/ppermute | solution.py:303
  7.8 7.2 %collective-permute-start.1 = (bf16[16,2,1024]{2,1,0:T(2,128)(2,1)S(1)}, bf16[16,2,1024]{2,1,0:T(2,128)(2,1)S(1)}, u32[]{:S(2)}, u32[]{:S(2)}) collective-permute-start(bf16[16,2,1024]{2,1,0:T(2,128)(2,1)S(1)} %get-tuple-element.15), channel_id=1, source_target_pairs={{0,4},{4,0},{8,12},{12,8},{16,20},{20,16},{24,28},{28,24},{1,5},{5... | collective-permute-start | bytes 196616 | tf_op jit(solution)/shard_map/ppermute | solution.py:303
  9.6 7.7 %collective-permute-start.2 = (bf16[16,2,1024]{2,1,0:T(2,128)(2,1)S(1)}, bf16[16,2,1024]{2,1,0:T(2,128)(2,1)S(1)}, u32[]{:S(2)}, u32[]{:S(2)}) collective-permute-start(bf16[16,2,1024]{2,1,0:T(2,128)(2,1)S(1)} %get-tuple-element.33), channel_id=1, source_target_pairs={{0,24},{4,28},{8,16},{12,20},{16,8},{20,12},{24,0},{28,4},{1,25},{... | collective-permute-start | bytes 196616 | tf_op jit(solution)/shard_map/ppermute | solution.py:303
  9.7 7.9 %collective-permute-start.6 = (bf16[16,2,1024]{2,1,0:T(2,128)(2,1)S(1)}, bf16[16,2,1024]{2,1,0:T(2,128)(2,1)S(1)}, u32[]{:S(2)}, u32[]{:S(2)}) collective-permute-start(bf16[16,2,1024]{2,1,0:T(2,128)(2,1)S(1)} %get-tuple-element.28), channel_id=1, source_target_pairs={{0,8},{4,12},{8,0},{12,4},{16,24},{20,28},{24,16},{28,20},{1,9},{5... | collective-permute-start | bytes 196616 | tf_op jit(solution)/shard_map/ppermute | solution.py:303
  9.7 8.0 %collective-permute-start.5 = (bf16[16,2,1024]{2,1,0:T(2,128)(2,1)S(1)}, bf16[16,2,1024]{2,1,0:T(2,128)(2,1)S(1)}, u32[]{:S(2)}, u32[]{:S(2)}) collective-permute-start(bf16[16,2,1024]{2,1,0:T(2,128)(2,1)S(1)} %get-tuple-element.29), channel_id=1, source_target_pairs={{0,20},{4,16},{8,28},{12,24},{16,4},{20,0},{24,12},{28,8},{1,21},{... | collective-permute-start | bytes 196616 | tf_op jit(solution)/shard_map/ppermute | solution.py:303
  14.9 5.2 %collective-permute-start.4 = (bf16[16,2,1024]{2,1,0:T(2,128)(2,1)S(1)}, bf16[16,2,1024]{2,1,0:T(2,128)(2,1)S(1)}, u32[]{:S(2)}, u32[]{:S(2)}) collective-permute-start(bf16[16,2,1024]{2,1,0:T(2,128)(2,1)S(1)} %get-tuple-element.30), channel_id=1, source_target_pairs={{0,12},{4,8},{8,4},{12,0},{16,28},{20,24},{24,20},{28,16},{1,13},{... | collective-permute-start | bytes 196616 | tf_op jit(solution)/shard_map/ppermute | solution.py:303
  15.0 5.2 %collective-permute-start.3 = (bf16[16,2,1024]{2,1,0:T(2,128)(2,1)S(1)}, bf16[16,2,1024]{2,1,0:T(2,128)(2,1)S(1)}, u32[]{:S(2)}, u32[]{:S(2)}) collective-permute-start(bf16[16,2,1024]{2,1,0:T(2,128)(2,1)S(1)} %get-tuple-element.31), channel_id=1, source_target_pairs={{0,16},{4,20},{8,24},{12,28},{16,0},{20,4},{24,8},{28,12},{1,17},{... | collective-permute-start | bytes 196616 | tf_op jit(solution)/shard_map/ppermute | solution.py:303
  35.2 11.0 %all-to-all-start.1 = ((bf16[32,9,2,128]{3,2,1,0:T(2,128)(2,1)}), bf16[32,9,2,128]{3,2,1,0:T(2,128)(2,1)S(1)}, u32[]{:S(2)}, u32[]{:S(2)}) async-start(bf16[32,9,2,128]{3,2,1,0:T(2,128)(2,1)} %bitcast.39), calls=%async_computation.1 | async-start | bytes 294912 | tf_op jit(solution)/shard_map/all_to_all | solution.py:338

commit v3 on v2

--- a/solution.py
+++ b/solution.py
@@ -313,7 +313,7 @@
         [x[step] for step in given] + [pick],
         flops=2 * 256 * 384 * cells,
     )
-    given = [step for step in order[::-1] if step // 2 in last]
+    given = [step for step in order[-2:] + order[-3::-1] if step // 2 in last]
     rows = -(-TERM_ROWS // (devices * 2)) * 2
     act, terms = call(
         functools.partial(layer_kernel, first, last, given),

time: 47.4 us -> 47.4 us (level)
  waiting for transfers between devices: 9 us -> 10.2 us
  blocking collectives: 12.5 us -> 11.4 us
    ppermute x7, waiting for transfers between devices: 2.57 us -> 3.74 us  [body(): lax.ppermute(block, 'space', [(source, source ^ step) for source in range...]
    all_to_all x1, blocking collectives: 12.5 us -> 11.4 us  [body(): mine = lax.all_to_all(blocks, axes, split_axis=0, concat_axis=0, tiled=True)]
  transfers between devices with their start and end apart: 8 -> 8, of which waited for: 4 -> 3; matrix products, arithmetic and copies ran while one was open for 6% -> 6% of each run, Pallas kernels for 5% -> 5%
where the time goes in v3:
time: 47.4 us; the launch traced here: 47.2 us
  starting transfers between devices  15.2 us (32%)
  blocking collectives  11.4 us (24%)
  waiting for transfers between devices  10.2 us (22%)
  Pallas kernels  6.01 us (13%)
  local copies, waits for them, and re-layouts  3.65 us (8%)
  between operations  0.8 us (2%)
    ppermute x7, starting transfers between devices, body(): lax.ppermute(block, 'space', [(source, source ^ step) for source in range...  12.6 us
    all_to_all x1, blocking collectives, body(): mine = lax.all_to_all(blocks, axes, split_axis=0, concat_axis=0, tiled=True)  11.4 us
    all_to_all x1, waiting for transfers between devices, body(): lax.all_to_all(spread, axes, split_axis=0, concat_axis=0, tiled=True)  6.43 us
    pallas_call x5, Pallas kernels, call(): pl.pallas_call(kernel, out_shape=tuple(outs), in_specs=[scalar if a.dtype...  5.05 us
    ppermute x7, waiting for transfers between devices, body(): lax.ppermute(block, 'space', [(source, source ^ step) for source in range...  3.74 us
    all_to_all x1, starting transfers between devices, body(): lax.all_to_all(spread, axes, split_axis=0, concat_axis=0, tiled=True)  2.58 us
    squeeze x1, local copies, waits for them, and re-layouts, body(): block = lax.dynamic_index_in_dim(rest, position ^ step, 0, keepdims=False)  1.27 us
    squeeze x1, local copies, waits for them, and re-layouts, body(): lax.dynamic_index_in_dim(crops, position ^ step, 0, keepdims=False)  1.04 us
  transfers between devices with their start and end apart: 8, of which 3 were waited for; matrix products, arithmetic and copies ran while one was open for 6% of the time, Pallas kernels for 5%

profile of v3, /device:TPU:0, one launch (start us, length us, event | category | flops | bytes accessed | tf_op | source)
XLA Modules:
  0.0 47.2 jit_solution(15236040675813004724)
XLA Ops:
  0.7 1.0 %dynamic-slice_bitcast_fusion.5 = (bf16[16,2,1024]{2,1,0:T(2,128)(2,1)S(1)}, bf16[16,2,1024]{2,1,0:T(2,128)(2,1)S(1)}) fusion(bf16[8,16,2,1024]{3,2,1,0:T(2,128)(2,1)} %param.4, s32[]{:T(128)S(6)} %select_n.26, s32[]{:T(128)S(6)} %select_n.25), kind=kLoop, calls=%fused_computation.5 | loop fusion | bytes 262152 | tf_op jit(solution)/shard_map/jit(dynamic_index_in_dim)/squeeze | solution.py:295
  1.7 6.0 %collective-permute-start = (bf16[16,2,1024]{2,1,0:T(2,128)(2,1)S(1)}, bf16[16,2,1024]{2,1,0:T(2,128)(2,1)S(1)}, u32[]{:S(2)}, u32[]{:S(2)}) collective-permute-start(bf16[16,2,1024]{2,1,0:T(2,128)(2,1)S(1)} %get-tuple-element.14), channel_id=1, source_target_pairs={{0,28},{4,24},{8,20},{12,16},{16,12},{20,8},{24,4},{28,0},{1,29},{... | collective-permute-start | bytes 196616 | tf_op jit(solution)/shard_map/ppermute | solution.py:303
  7.8 0.5 %collective-permute-start.1 = (bf16[16,2,1024]{2,1,0:T(2,128)(2,1)S(1)}, bf16[16,2,1024]{2,1,0:T(2,128)(2,1)S(1)}, u32[]{:S(2)}, u32[]{:S(2)}) collective-permute-start(bf16[16,2,1024]{2,1,0:T(2,128)(2,1)S(1)} %get-tuple-element.15), channel_id=1, source_target_pairs={{0,4},{4,0},{8,12},{12,8},{16,20},{20,16},{24,28},{28,24},{1,5},{5... | collective-permute-start | bytes 196616 | tf_op jit(solution)/shard_map/ppermute | solution.py:303
  8.3 1.3 %dynamic-slice_bitcast_fusion = (bf16[16,2,1024]{2,1,0:T(2,128)(2,1)S(1)}, bf16[16,2,1024]{2,1,0:T(2,128)(2,1)S(1)}, bf16[16,2,1024]{2,1,0:T(2,128)(2,1)S(1)}, b...) fusion(bf16[8,16,2,1024]{3,2,1,0:T(2,128)(2,1)} %param.4, ...), kind=kLoop, calls=%fused_computation | loop fusion | bytes 786456 | tf_op jit(solution)/shard_map/jit(dynamic_index_in_dim)/squeeze | solution.py:301
  9.6 0.2 collective-permute-start.2
  9.7 5.2 %collective-permute-start.5 = (bf16[16,2,1024]{2,1,0:T(2,128)(2,1)S(1)}, bf16[16,2,1024]{2,1,0:T(2,128)(2,1)S(1)}, u32[]{:S(2)}, u32[]{:S(2)}) collective-permute-start(bf16[16,2,1024]{2,1,0:T(2,128)(2,1)S(1)} %get-tuple-element.29), channel_id=1, source_target_pairs={{0,20},{4,16},{8,28},{12,24},{16,4},{20,0},{24,12},{28,8},{1,21},{... | collective-permute-start | bytes 196616 | tf_op jit(solution)/shard_map/ppermute | solution.py:303
  15.0 0.6 %collective-permute-start.3 = (bf16[16,2,1024]{2,1,0:T(2,128)(2,1)S(1)}, bf16[16,2,1024]{2,1,0:T(2,128)(2,1)S(1)}, u32[]{:S(2)}, u32[]{:S(2)}) collective-permute-start(bf16[16,2,1024]{2,1,0:T(2,128)(2,1)S(1)} %get-tuple-element.31), channel_id=1, source_target_pairs={{0,12},{4,8},{8,4},{12,0},{16,28},{20,24},{24,20},{28,16},{1,13},{... | collective-permute-start | bytes 196616 | tf_op jit(solution)/shard_map/ppermute | solution.py:303
  15.6 0.1 copy.9
  15.8 0.1 reshape.88
  15.9 0.1 copy.11.og_ref
  16.0 1.3 %shard_map.67 = (bf16[384,384]{1,0:T(8,128)(2,1)S(1)}, bf16[256,768]{1,0:T(8,128)(2,1)S(1)}, bf16[512,1152]{1,0:T(8,128)(2,1)S(1)}, bf16[128,512]{1,0:T(8,128)(2,1)S(1)}) custom-call(bf16[3,3,3,16,32]{4,3,2,1,0:T(8,128)(2,1)S(1)} %bitcast.84, bf16[3,3,3,32,64]{4,3,2,1,0:T(8,128)(2,1)S(1)} %bitcast.82, bf16[128,128]{1,0:T(8,128)(2,1)S(1)} %copy.11.og_ref), custom_call_target="tpu_custom_call" | custom-call | flops 301989888 | bytes 2169856 | tf_op jit(solution)/shard_map/pallas_call | solution.py:246
  17.3 0.3 shard_map.68.y_ref
  17.6 2.7 %collective-permute-done.5 = bf16[16,2,1024]{2,1,0:T(2,128)(2,1)S(1)} collective-permute-done((bf16[16,2,1024]{2,1,0:T(2,128)(2,1)S(1)}, bf16[16,2,1024]{2,1,0:T(2,128)(2,1)S(1)}, u32[]{:S(2)}, u32[]{:S(2)}) %collective-permute-start.5) | collective-permute-done | bytes 65568 | tf_op jit(solution)/shard_map/ppermute | solution.py:303
  20.4 1.0 %collective-permute-done.3 = bf16[16,2,1024]{2,1,0:T(2,128)(2,1)S(1)} collective-permute-done((bf16[16,2,1024]{2,1,0:T(2,128)(2,1)S(1)}, bf16[16,2,1024]{2,1,0:T(2,128)(2,1)S(1)}, u32[]{:S(2)}, u32[]{:S(2)}) %collective-permute-start.3) | collective-permute-done | bytes 65568 | tf_op jit(solution)/shard_map/ppermute | solution.py:303
  21.4 1.8 %shard_map.69 = (bf16[128,512]{1,0:T(8,128)(2,1)S(1)}, bf16[576,128]{1,0:T(8,128)(2,1)S(1)}) custom-call(bf16[768,256]{1,0:T(8,128)(2,1)S(1)} %shard_map.68.y_ref, bf16[256,128]{1,0:T(8,128)(2,1)S(1)} %bitcast.81, bf16[256,128]{1,0:T(8,128)(2,1)S(1)} %bitcast.80, bf16[256,128]{1,0:T(8,128)(2,1)S(1)} %bitcast.79, bf16[256,128]{1,0:T(8,128)(2,1)S(1)} %bitcast.78, ...), custom_call_target="tpu_custom_call" | custom-call | flops 536870912 | bytes 2932736 | tf_op jit(solution)/shard_map/pallas_call | solution.py:246
  23.1 11.4 %all_to_all.10 = bf16[32,9,2,128]{3,2,1,0:T(2,128)(2,1)S(1)} all-to-all(bf16[32,9,2,128]{3,2,1,0:T(2,128)(2,1)S(1)} %bitcast.74), channel_id=1, replica_groups=mesh['space'=8,'sample'=4] {'space','sample'}, dimensions={0} | all-to-all | bytes 294912 | tf_op jit(solution)/shard_map/all_to_all | solution.py:326
  34.5 0.7 %shard_map.71 = bf16[576,128]{1,0:T(8,128)(2,1)} custom-call(bf16[576,128]{1,0:T(8,128)(2,1)S(1)} %bitcast.72), custom_call_target="tpu_custom_call" | custom-call | bytes 294912 | tf_op jit(solution)/shard_map/pallas_call | solution.py:246
  35.2 2.6 %all-to-all-start.1 = ((bf16[32,9,2,128]{3,2,1,0:T(2,128)(2,1)}), bf16[32,9,2,128]{3,2,1,0:T(2,128)(2,1)S(1)}, u32[]{:S(2)}, u32[]{:S(2)}) async-start(bf16[32,9,2,128]{3,2,1,0:T(2,128)(2,1)} %bitcast.39), calls=%async_computation.1 | async-start | bytes 294912 | tf_op jit(solution)/shard_map/all_to_all | solution.py:338
  37.8 1.0 %shard_map.70 = bf16[128,128]{1,0:T(8,128)(2,1)S(1)} custom-call(bf16[128,512]{1,0:T(8,128)(2,1)S(1)} %get-tuple-element.21.act_ref, bf16[3,3,3,32,64]{4,3,2,1,0:T(8,128)(2,1)S(1)} %bitcast.83), custom_call_target="tpu_custom_call" | custom-call | flops 150994944 | bytes 274432 | tf_op jit(solution)/shard_map/pallas_call | solution.py:246
  38.8 0.1 copy.12
  38.9 0.1 reshape.97
  39.1 0.7 %copy.14 = bf16[1,64,4,64]{3,2,1,0:T(4,128)(2,1)} copy(bf16[1,64,4,64]{1,3,2,0:T(8,128)(2,1)S(1)} %bitcast.86) | data formatting | bytes 65536
  39.8 6.4 %all-to-all-done.1 = bf16[32,9,2,128]{3,2,1,0:T(2,128)(2,1)S(1)} async-done(((bf16[32,9,2,128]{3,2,1,0:T(2,128)(2,1)}), bf16[32,9,2,128]{3,2,1,0:T(2,128)(2,1)S(1)}, u32[]{:S(2)}, u32[]{:S(2)}) %all-to-all-start.1) | async-done | bytes 147488 | tf_op jit(solution)/shard_map/all_to_all | solution.py:338
  46.2 1.0 %shard_map.72 = (f32[3,3,3,16,32]{4,3,2,1,0:T(8,128)}, f32[3,3,3,32,64]{4,3,2,1,0:T(8,128)}) custom-call(bf16[576,128]{1,0:T(8,128)(2,1)S(1)} %bitcast.71), custom_call_target="tpu_custom_call" | custom-call | tf_op jit(solution)/shard_map/pallas_call | solution.py:340
  (15 shorter events, 0.1 us)
Async XLA Ops:
  0.6 15.0 %copy-start.2 = (bf16[1,64,4,64]{3,2,1,0:T(4,128)(2,1)S(1)}, bf16[1,64,4,64]{3,2,1,0:T(4,128)(2,1)}, u32[]{:S(2)}) copy-start(bf16[1,64,4,64]{3,2,1,0:T(4,128)(2,1)} %param.7) | copy-start | bytes 98308
  0.6 15.4 %copy-start = (bf16[64,32,3,3,3]{0,1,4,3,2:T(8,128)(2,1)S(1)}, bf16[64,32,3,3,3]{0,1,4,3,2:T(8,128)(2,1)}, u32[]{:S(2)}) copy-start(bf16[64,32,3,3,3]{0,1,4,3,2:T(8,128)(2,1)} %param.6) | copy-start | bytes 331780
  0.7 15.4 %copy-start.1 = (bf16[32,16,3,3,3]{0,1,4,3,2:T(8,128)(2,1)S(1)}, bf16[32,16,3,3,3]{0,1,4,3,2:T(8,128)(2,1)}, u32[]{:S(2)}) copy-start(bf16[32,16,3,3,3]{0,1,4,3,2:T(8,128)(2,1)} %param.5) | copy-start | bytes 82948
  1.7 13.2 %collective-permute-start = (bf16[16,2,1024]{2,1,0:T(2,128)(2,1)S(1)}, bf16[16,2,1024]{2,1,0:T(2,128)(2,1)S(1)}, u32[]{:S(2)}, u32[]{:S(2)}) collective-permute-start(bf16[16,2,1024]{2,1,0:T(2,128)(2,1)S(1)} %get-tuple-element.14), channel_id=1, source_target_pairs={{0,28},{4,24},{8,20},{12,16},{16,12},{20,8},{24,4},{28,0},{1,29},{... | collective-permute-start | bytes 196616 | tf_op jit(solution)/shard_map/ppermute | solution.py:303
  7.8 7.2 %collective-permute-start.1 = (bf16[16,2,1024]{2,1,0:T(2,128)(2,1)S(1)}, bf16[16,2,1024]{2,1,0:T(2,128)(2,1)S(1)}, u32[]{:S(2)}, u32[]{:S(2)}) collective-permute-start(bf16[16,2,1024]{2,1,0:T(2,128)(2,1)S(1)} %get-tuple-element.15), channel_id=1, source_target_pairs={{0,4},{4,0},{8,12},{12,8},{16,20},{20,16},{24,28},{28,24},{1,5},{5... | collective-permute-start | bytes 196616 | tf_op jit(solution)/shard_map/ppermute | solution.py:303
  9.6 7.7 %collective-permute-start.2 = (bf16[16,2,1024]{2,1,0:T(2,128)(2,1)S(1)}, bf16[16,2,1024]{2,1,0:T(2,128)(2,1)S(1)}, u32[]{:S(2)}, u32[]{:S(2)}) collective-permute-start(bf16[16,2,1024]{2,1,0:T(2,128)(2,1)S(1)} %get-tuple-element.33), channel_id=1, source_target_pairs={{0,24},{4,28},{8,16},{12,20},{16,8},{20,12},{24,0},{28,4},{1,25},{... | collective-permute-start | bytes 196616 | tf_op jit(solution)/shard_map/ppermute | solution.py:303
  9.7 7.9 %collective-permute-start.6 = (bf16[16,2,1024]{2,1,0:T(2,128)(2,1)S(1)}, bf16[16,2,1024]{2,1,0:T(2,128)(2,1)S(1)}, u32[]{:S(2)}, u32[]{:S(2)}) collective-permute-start(bf16[16,2,1024]{2,1,0:T(2,128)(2,1)S(1)} %get-tuple-element.28), channel_id=1, source_target_pairs={{0,8},{4,12},{8,0},{12,4},{16,24},{20,28},{24,16},{28,20},{1,9},{5... | collective-permute-start | bytes 196616 | tf_op jit(solution)/shard_map/ppermute | solution.py:303
  9.7 10.6 %collective-permute-start.5 = (bf16[16,2,1024]{2,1,0:T(2,128)(2,1)S(1)}, bf16[16,2,1024]{2,1,0:T(2,128)(2,1)S(1)}, u32[]{:S(2)}, u32[]{:S(2)}) collective-permute-start(bf16[16,2,1024]{2,1,0:T(2,128)(2,1)S(1)} %get-tuple-element.29), channel_id=1, source_target_pairs={{0,20},{4,16},{8,28},{12,24},{16,4},{20,0},{24,12},{28,8},{1,21},{... | collective-permute-start | bytes 196616 | tf_op jit(solution)/shard_map/ppermute | solution.py:303
  14.9 5.4 %collective-permute-start.4 = (bf16[16,2,1024]{2,1,0:T(2,128)(2,1)S(1)}, bf16[16,2,1024]{2,1,0:T(2,128)(2,1)S(1)}, u32[]{:S(2)}, u32[]{:S(2)}) collective-permute-start(bf16[16,2,1024]{2,1,0:T(2,128)(2,1)S(1)} %get-tuple-element.30), channel_id=1, source_target_pairs={{0,16},{4,20},{8,24},{12,28},{16,0},{20,4},{24,8},{28,12},{1,17},{... | collective-permute-start | bytes 196616 | tf_op jit(solution)/shard_map/ppermute | solution.py:303
  15.0 6.4 %collective-permute-start.3 = (bf16[16,2,1024]{2,1,0:T(2,128)(2,1)S(1)}, bf16[16,2,1024]{2,1,0:T(2,128)(2,1)S(1)}, u32[]{:S(2)}, u32[]{:S(2)}) collective-permute-start(bf16[16,2,1024]{2,1,0:T(2,128)(2,1)S(1)} %get-tuple-element.31), channel_id=1, source_target_pairs={{0,12},{4,8},{8,4},{12,0},{16,28},{20,24},{24,20},{28,16},{1,13},{... | collective-permute-start | bytes 196616 | tf_op jit(solution)/shard_map/ppermute | solution.py:303
  35.2 11.0 %all-to-all-start.1 = ((bf16[32,9,2,128]{3,2,1,0:T(2,128)(2,1)}), bf16[32,9,2,128]{3,2,1,0:T(2,128)(2,1)S(1)}, u32[]{:S(2)}, u32[]{:S(2)}) async-start(bf16[32,9,2,128]{3,2,1,0:T(2,128)(2,1)} %bitcast.39), calls=%async_computation.1 | async-start | bytes 294912 | tf_op jit(solution)/shard_map/all_to_all | solution.py:338
